TPU v7x, 256 devices: a whole 4x4x8 slice. The times are simulated.
256 devices in a mesh: row: 16 (over z, y_hi), col: 16 (over x, y_lo, core).
Axes of the slice: x: 4, y: 4 (y_hi: 2, y_lo: 2; y = y_hi * 2 + y_lo), z: 8, core: 2. Of those that a mesh axis runs over, the one named last changes fastest.
Arguments:
- amplitudes: float32 [512, 512], P(('col', 'row')), may hold values from -6 to 6
- integrals: float32 [512, 184320], P('col', 'row'), may hold values from -0.25 to 0.25
- previous: float32 [512, 184320], P('col', 'row'), may hold values from -6 to 6
Outputs:
- residual: float32 [512, 184320], P('col', 'row')
All inputs are finite; a program needn't handle non-finite values.
Results may differ from a plain program's by a relative error of at most 0.000051.
Values sent between devices are 32-bit elements; how exact they have to be, the bound alone decides.
No kernel may reach another device: no remote copies, remote signals or barrier semaphores. Data moves between devices by JAX's collectives and lax.ppermute only.
A program may use at most 128 MiB of HBM per device.

v0:
```python
import jax
import jax.numpy as jnp
from jax import lax
from jax.sharding import PartitionSpec as P


def body(amplitudes, integrals, previous):
    cd_major = lax.all_to_all(amplitudes, "row", split_axis=1, concat_axis=0, tiled=True)
    panels = lax.all_gather(cd_major, "row", axis=1, tiled=True)
    product = jnp.dot(
        panels,
        lax.all_gather(integrals, "col", axis=0, tiled=True),
        precision=lax.Precision.HIGHEST,
        preferred_element_type=jnp.float32,
    )
    return previous + product


def solution(mesh):
    in_specs = (P(("col", "row"), None), P("col", "row"), P("col", "row"))
    out_specs = P("col", "row")
    return jax.shard_map(body, mesh=mesh, in_specs=in_specs, out_specs=out_specs, check_vma=False)
```

profile of v0, /device:TPU:1, one launch (start us, length us, event | category | flops | bytes accessed | tf_op | source)
XLA Modules:
  0.0 171.0 jit_solution(5167270141869506396)
XLA Ops:
  6.5 0.0 copy-start.1
  6.5 0.0 copy-start
  6.5 0.0 all-gather.2.cloned.1.call-start
  6.5 0.7 all-gather.2.cloned.1.call-update
  7.3 0.0 copy-done.1
  7.3 0.1 all_to_all.14
  7.4 20.5 %all_to_all.19 = f32[2,16,32]{2,0,1:T(2,128)S(1)} all-to-all(f32[2,16,32]{2,0,1:T(2,128)S(1)} %copy.5), channel_id=1, replica_groups=mesh['row'=16,'col'=16] {'row'}, dimensions={1} | all-to-all | bytes 8192 | tf_op jit(solution)/shard_map/all_to_all | solution.py:8
  27.8 0.1 copy.6
  27.9 31.4 %all_gather.6 = f32[32,512]{0,1:T(8,128)S(1)} all-gather(f32[32,32]{0,1:T(8,128)S(1)} %copy.6), channel_id=1, replica_groups=mesh['row'=16,'col'=16] {'row'}, dimensions={1}, use_global_device_ids=true | all-gather | bytes 69632 | tf_op jit(solution)/shard_map/all_gather | solution.py:9
  59.3 85.7 %all-gather.2.cloned.1.call-done = f32[512,11520]{1,0:T(8,128)} async-done(((f32[32,11520]{1,0:T(8,128)}), f32[512,11520]{1,0:T(8,128)}) %all-gather.2.cloned.1.call-update) | async-done | bytes 23592976 | tf_op jit(solution)/shard_map/all_gather | solution.py:12
  145.0 0.0 copy-done
  145.0 19.1 %convolution_add_fusion = f32[32,11520]{1,0:T(8,128)} fusion(f32[32,11520]{1,0:T(8,128)S(1)} %copy-done, f32[32,512]{0,1:T(8,128)S(1)} %all_gather.6, f32[512,11520]{1,0:T(8,128)} %all-gather.2.cloned.1.call-done), kind=kOutput, calls=%fused_computation | convolution fusion | flops 2265292800 | bytes 26607616 | tf_op jit(solution)/shard_map/dot_general | solution.py:10
  (1 shorter events, 0.0 us)
Async XLA Ops:
  6.5 0.7 copy-start.1
  6.5 138.5 %copy-start = (f32[32,11520]{1,0:T(8,128)S(1)}, f32[32,11520]{1,0:T(8,128)}, u32[]{:S(2)}) copy-start(f32[32,11520]{1,0:T(8,128)} %param.5) | copy-start | bytes 4423684
  6.5 138.5 %all-gather.2.cloned.1.call-start = ((), (), s32[]{:S(2)}) async-start(), calls=%async_computation.1 | async-start | bytes 25067520 | tf_op jit(solution)/shard_map/all_gather | solution.py:12
Sparse Core Ops, SparseCore 0:
  9.2 135.7 all-gather.1
where the time goes:
time: 171 us
  waiting for transfers between devices  86.4 us (51%)
  blocking collectives  51.8 us (30%)
  matrix products  19.1 us (11%)
  between operations  13.4 us (8%)
    all_gather x1, waiting for transfers between devices, body(): lax.all_gather(integrals, 'col', axis=0, tiled=True)  85.7 us
    all_gather x1, blocking collectives, body(): panels = lax.all_gather(cd_major, 'row', axis=1, tiled=True)  31.4 us
    all_to_all x1, blocking collectives, body(): lax.all_to_all(amplitudes, 'row', split_axis=1, concat_axis=0, tiled=True)  20.5 us
    dot_general x1, matrix products, body(): jnp.dot(panels, lax.all_gather(integrals, 'col', axis=0, tiled=True), pre...  19.1 us
  transfers between devices with their start and end apart: 1, of which 1 were waited for; matrix products, arithmetic and copies ran while one was open for 0% of the time, Pallas kernels for 0%

commit v1 on v0

v1 whole, which is shorter than its diff:
```python
import functools

import jax
import jax.numpy as jnp
from jax import lax
from jax.experimental import pallas as pl
from jax.experimental.pallas import tpu as pltpu
from jax.sharding import PartitionSpec as P

LANES = 128
ROWS = 32
TILES = 11
SPLIT = 8 * TILES * LANES
MSG = TILES * ROWS + 8
OFFSETS = [(dx, dy) for dx in range(4) for dy in range(2)]
ORDER = [1, 4, 3, 2, 7, 6, 5]
MIB = 1 << 20


def cols(f):
    pairs = []
    for c in range(16):
        x, y, k = f(c >> 2, (c >> 1) & 1, c & 1)
        pairs.append((c, 4 * (x % 4) + 2 * (y % 2) + k % 2))
    return pairs


def everywhere(f):
    pairs = []
    for d in range(256):
        r, c = d >> 4, d & 15
        x, y, z, k = f(c >> 2, 2 * (r & 1) + ((c >> 1) & 1), r >> 1, c & 1)
        x, y, z, k = x % 4, y % 4, z % 8, k % 2
        pairs.append((d, 16 * (2 * z + (y >> 1)) + 4 * x + 2 * (y & 1) + k))
    return pairs


def move(a, dx, dy):
    return lax.ppermute(a, "col", cols(lambda x, y, k: (x + dx, y + dy, k)))


def swap_cores(a):
    return lax.ppermute(a, "col", cols(lambda x, y, k: (x, y, k + 1)))


def shift(a, f):
    return lax.ppermute(a, ("row", "col"), everywhere(f))


def here():
    col, row = lax.axis_index("col"), lax.axis_index("row")
    return col // 4, (col // 2) % 2, col % 2, row


def chip(x, y, o, sign):
    dx, dy = OFFSETS[o]
    return 2 * ((x + 4 + sign * dx) % 4) + (y + dy) % 2


def split(a):
    hi = a.astype(jnp.bfloat16)
    return hi, (a - hi.astype(jnp.float32)).astype(jnp.bfloat16)


def lane_group():
    return lax.broadcasted_iota(jnp.int32, (8, LANES), 1) // ROWS


def pack_kernel(v, *msgs):
    x, y, _, _ = here()
    group = lane_group()
    for o, msg in enumerate(msgs):
        q = chip(x, y, o, 1)
        for t in range(TILES):
            at = pl.multiple_of((q * TILES + t) * LANES, LANES)
            msg[t * ROWS : (t + 1) * ROWS, :] = v[:, pl.ds(at, LANES)]
        at = pl.multiple_of(SPLIT + (q // 4) * LANES, LANES)
        folded = jnp.zeros((8, LANES), jnp.float32)
        for g in range(4):
            part = v[8 * g : 8 * g + 8, pl.ds(at, LANES)]
            part = pltpu.roll(part, (ROWS * (g + 4 - q % 4)) % LANES, 1)
            folded = jnp.where(group == g, part, folded)
        msg[TILES * ROWS :, :] = folded


def amplitudes_kernel(*refs):
    parts, (hi_out, lo_out) = refs[:4], refs[4:6]
    x, y_lo, k, row = here()
    y, z = 2 * (row % 2) + y_lo, row // 2
    s = lax.broadcasted_iota(jnp.int32, (256, 256), 1)
    d = lax.broadcasted_iota(jnp.int32, (256, 256), 0)
    i, jy, jx, j4, jz = s % 2, (s // 2) % 4, (s // 8) % 4, (s // 32) % 2, s // 64
    back = jnp.where(jz == 0, 0, jnp.where(jz == 1, 1, jnp.where(jz == 2, 7, jnp.where(k == 0, 2, 6))))
    from_x, from_y, from_z = (x + 4 - jx) % 4, (y + 4 - jy) % 4, (z + 16 - back - 4 * j4) % 8
    offset = 2 * ((from_x + 4 - x) % 4) + (from_y + y_lo) % 2
    target = offset * ROWS + 2 * (2 * from_z + from_y // 2) + i
    order = jnp.where(d == target, 1.0, 0.0).astype(jnp.bfloat16)
    for c in range(4):
        rows = jnp.concatenate([p[pl.ds(c, 64, stride=4), :] for p in parts], axis=0)
        for piece, out in zip(split(rows), (hi_out, lo_out)):
            out[:, c * LANES : (c + 1) * LANES] = jnp.dot(
                order, piece, preferred_element_type=jnp.float32
            ).astype(jnp.bfloat16)


def ladder_kernel(*refs):
    mine, other, (t_hi, t_lo) = refs[:8], refs[8:16], refs[16:18]
    msgs, (v_hi, v_lo) = refs[18:26], refs[26:28]
    x, y, k, _ = here()
    group = lane_group()
    for o in range(8):
        q = chip(x, y, o, -1)
        for core, blocks in ((k, mine), (1 - k, other)):
            at = pl.multiple_of((2 * q + core) * ROWS, ROWS)
            for t in range(TILES):
                hi, lo = split(blocks[o][t * ROWS : (t + 1) * ROWS, :])
                v_hi[pl.ds(at, ROWS), t * LANES : (t + 1) * LANES] = hi
                v_lo[pl.ds(at, ROWS), t * LANES : (t + 1) * LANES] = lo
            folded = blocks[o][TILES * ROWS :, :]
            rows = [folded] + [pltpu.roll(folded, LANES - ROWS * g, 1) for g in range(1, 4)]
            hi, lo = split(jnp.concatenate(rows, axis=0))
            v_hi[pl.ds(at, ROWS), TILES * LANES :] = hi
            v_lo[pl.ds(at, ROWS), TILES * LANES :] = lo
    dot = functools.partial(jnp.dot, preferred_element_type=jnp.float32)
    for j in range(6):
        lanes = slice(2 * j * LANES, (2 * j + 2) * LANES)
        hi, lo = v_hi[:, lanes], v_lo[:, lanes]
        out = dot(t_hi[...], hi) + (dot(t_hi[...], lo) + dot(t_lo[...], hi))
        for o in range(8):
            rows = out[o * ROWS : (o + 1) * ROWS]
            msgs[o][2 * j * ROWS : (2 * j + 1) * ROWS, :] = rows[:, :LANES]
            if j < 5:
                msgs[o][(2 * j + 1) * ROWS : (2 * j + 2) * ROWS, :] = rows[:, LANES:]
            else:
                folded = rows[:8, LANES:]
                for g in range(1, 4):
                    part = pltpu.roll(rows[8 * g : 8 * g + 8, LANES:], ROWS * g, 1)
                    folded = jnp.where(group == g, part, folded)
                msgs[o][TILES * ROWS :, :] = folded


def add_kernel(*refs):
    msgs, previous, out = refs[:8], refs[8], refs[9]
    x, y, _, _ = here()
    group = lane_group()
    narrow = [[jnp.zeros((8, LANES), jnp.float32) for _ in range(4)] for _ in range(2)]
    for o in range(8):
        q = chip(x, y, o, -1)
        for t in range(TILES):
            at = pl.ds(pl.multiple_of((q * TILES + t) * LANES, LANES), LANES)
            out[:, at] = previous[:, at] + msgs[o][t * ROWS : (t + 1) * ROWS, :]
        folded = msgs[o][TILES * ROWS :, :]
        for g in range(4):
            part = pltpu.roll(folded, (ROWS * (q % 4 + 4 - g)) % LANES, 1)
            for j in range(2):
                narrow[j][g] = jnp.where(group + 4 * j == q, part, narrow[j][g])
    for j in range(2):
        at = slice(SPLIT + j * LANES, SPLIT + (j + 1) * LANES)
        out[:, at] = previous[:, at] + jnp.concatenate(narrow[j], axis=0)


def call(kernel, outs, args, flops=0, scratch=(), limit=16):
    moved = sum(a.size * a.dtype.itemsize for a in list(args) + list(outs))
    return pl.pallas_call(
        kernel,
        out_shape=outs,
        in_specs=[pl.BlockSpec(memory_space=pltpu.VMEM)] * len(args),
        out_specs=jax.tree.map(lambda _: pl.BlockSpec(memory_space=pltpu.VMEM), outs),
        scratch_shapes=list(scratch),
        compiler_params=pltpu.CompilerParams(vmem_limit_bytes=limit * MIB),
        cost_estimate=pl.CostEstimate(flops=flops, bytes_accessed=moved, transcendentals=0),
    )(*args)


def gather_amplitudes(a):
    part = a.reshape(8, LANES)
    part = jnp.concatenate([part] + [shift(part, lambda x, y, z, k, j=j: (x, y + j, z, k)) for j in range(1, 4)], 0)
    part = jnp.concatenate([part] + [shift(part, lambda x, y, z, k, j=j: (x + j, y, z, k)) for j in range(1, 4)], 0)
    part = jnp.concatenate([part, shift(part, lambda x, y, z, k: (x, y, z + 4, k))], 0)
    return [
        part,
        shift(part, lambda x, y, z, k: (x, y, z + 1, k)),
        shift(part, lambda x, y, z, k: (x, y, z - 1, k)),
        shift(part, lambda x, y, z, k: (x, y, z + 2 - 4 * k, k)),
    ]


def body(amplitudes, integrals, previous):
    msg = jax.ShapeDtypeStruct((MSG, LANES), jnp.float32)
    t_shape = jax.ShapeDtypeStruct((256, 512), jnp.bfloat16)
    sent = call(pack_kernel, [msg] * 8, [integrals])
    mine = {0: sent[0]}
    for o in ORDER:
        mine[o] = move(sent[o], *OFFSETS[o])
    mine = [mine[o] for o in range(8)]
    other = [swap_cores(m) for m in mine]
    t_hi, t_lo = call(amplitudes_kernel, [t_shape] * 2, gather_amplitudes(amplitudes), 2 * 256 * 256 * 1024)
    sent = call(
        ladder_kernel,
        [msg] * 8,
        mine + other + [t_hi, t_lo],
        3 * 2 * 256 * 512 * 1440,
        [pltpu.VMEM((512, 12 * LANES), jnp.bfloat16)] * 2,
        24,
    )
    back = {0: sent[0]}
    for o in ORDER:
        back[o] = move(sent[o], *OFFSETS[o])
    out = jax.ShapeDtypeStruct(previous.shape, jnp.float32)
    return call(add_kernel, [out], [back[o] for o in range(8)] + [previous])[0]


def solution(mesh):
    in_specs = (P(("col", "row"), None), P("col", "row"), P("col", "row"))
    out_specs = P("col", "row")
    return jax.shard_map(body, mesh=mesh, in_specs=in_specs, out_specs=out_specs, check_vma=False)
```

time: 171 us -> 85.2 us (0.50)
  the two profiles are of different devices: /device:TPU:1 before, /device:TPU:2 now
where the time goes in v1:
time: 85.2 us; the launch traced here: 84.2 us
  starting transfers between devices  42.9 us (50%)
  waiting for transfers between devices  34.8 us (41%)
  Pallas kernels  4.32 us (5%)
  local copies, waits for them, and re-layouts  2.1 us (2%)
    ppermute x14, starting transfers between devices, move(): return lax.ppermute(a, 'col', cols(lambda x, y, k: (x + dx, y + dy, k)))  21 us
    ppermute x10, starting transfers between devices, shift(): return lax.ppermute(a, ('row', 'col'), everywhere(f))  20.9 us
    ppermute x14, waiting for transfers between devices, move(): return lax.ppermute(a, 'col', cols(lambda x, y, k: (x + dx, y + dy, k)))  19.5 us
    ppermute x10, waiting for transfers between devices, shift(): return lax.ppermute(a, ('row', 'col'), everywhere(f))  14.4 us
    pallas_call x4, Pallas kernels, call(): pl.pallas_call(kernel, out_shape=outs, in_specs=[pl.BlockSpec(memory_spac...  4.32 us
  transfers between devices with their start and end apart: 32, of which 18 were waited for; matrix products, arithmetic and copies ran while one was open for 0% of the time, Pallas kernels for 1%

profile of v1, /device:TPU:2, one launch (start us, length us, event | category | flops | bytes accessed | tf_op | source)
XLA Modules:
  0.0 84.2 jit_solution(12714576497123570925)
XLA Ops:
  0.7 3.0 %collective-permute-start.17 = (f32[8,128]{1,0:T(8,128)S(1)}, f32[8,128]{1,0:T(8,128)S(1)}, u32[]{:S(2)}, u32[]{:S(2)}) collective-permute-start(f32[8,128]{1,0:T(8,128)S(1)} %reshape.3), channel_id=1, source_target_pairs={{0,18},{1,19},{2,0},{3,1},{4,22},{5,23},{6,4},{7,5},{8,26},{9,27},... | collective-permute-start | bytes 12296 | tf_op jit(solution)/shard_map/ppermute | solution.py:47
  5.3 3.8 %collective-permute-done.15 = f32[8,128]{1,0:T(8,128)S(1)} collective-permute-done((f32[8,128]{1,0:T(8,128)S(1)}, f32[8,128]{1,0:T(8,128)S(1)}, u32[]{:S(2)}, u32[]{:S(2)}) %collective-permute-start.15) | collective-permute-done | bytes 4128 | tf_op jit(solution)/shard_map/ppermute | solution.py:47
  9.2 1.6 %collective-permute-start.18 = (f32[32,128]{1,0:T(8,128)S(1)}, f32[32,128]{1,0:T(8,128)S(1)}, u32[]{:S(2)}, u32[]{:S(2)}) collective-permute-start(f32[32,128]{1,0:T(8,128)S(1)} %get-tuple-element.49), channel_id=1, source_target_pairs={{0,4},{1,5},{2,6},{3,7},{4,8},{5,9},{6,10},{7,11},{8,12},{9,13},{1... | collective-permute-start | bytes 49160 | tf_op jit(solution)/shard_map/ppermute | solution.py:47
  10.8 1.4 %copy-done = f32[32,11520]{1,0:T(8,128)S(1)} copy-done((f32[32,11520]{1,0:T(8,128)S(1)}, f32[32,11520]{1,0:T(8,128)}, u32[]{:S(2)}) %copy-start) | copy-done | bytes 1474584
  12.5 1.3 %collective-permute-start.1 = (f32[360,128]{1,0:T(8,128)S(1)}, f32[360,128]{1,0:T(8,128)S(1)}, u32[]{:S(2)}, u32[]{:S(2)}) collective-permute-start(f32[360,128]{1,0:T(8,128)S(1)} %get-tuple-element.25), channel_id=1, source_target_pairs={{0,4},{1,5},{2,6},{3,7},{4,8},{5,9},{6,10},{7,11},{8,12},{9,13},{1... | collective-permute-start | bytes 552968 | tf_op jit(solution)/shard_map/ppermute | solution.py:39
  13.8 1.8 %collective-permute-start.2 = (f32[360,128]{1,0:T(8,128)S(1)}, f32[360,128]{1,0:T(8,128)S(1)}, u32[]{:S(2)}, u32[]{:S(2)}) collective-permute-start(f32[360,128]{1,0:T(8,128)S(1)} %get-tuple-element.26), channel_id=1, source_target_pairs={{0,6},{1,7},{2,4},{3,5},{4,10},{5,11},{6,8},{7,9},{8,14},{9,15},{1... | collective-permute-start | bytes 552968 | tf_op jit(solution)/shard_map/ppermute | solution.py:39
  15.7 1.5 %collective-permute-start.20 = (f32[32,128]{1,0:T(8,128)S(1)}, f32[32,128]{1,0:T(8,128)S(1)}, u32[]{:S(2)}, u32[]{:S(2)}) collective-permute-start(f32[32,128]{1,0:T(8,128)S(1)} %get-tuple-element.49), channel_id=1, source_target_pairs={{0,12},{1,13},{2,14},{3,15},{4,0},{5,1},{6,2},{7,3},{8,4},{9,5},{1... | collective-permute-start | bytes 49160 | tf_op jit(solution)/shard_map/ppermute | solution.py:47
  17.2 1.4 %collective-permute-start.19 = (f32[32,128]{1,0:T(8,128)S(1)}, f32[32,128]{1,0:T(8,128)S(1)}, u32[]{:S(2)}, u32[]{:S(2)}) collective-permute-start(f32[32,128]{1,0:T(8,128)S(1)} %get-tuple-element.49), channel_id=1, source_target_pairs={{0,8},{1,9},{2,10},{3,11},{4,12},{5,13},{6,14},{7,15},{8,0},{9,1},... | collective-permute-start | bytes 49160 | tf_op jit(solution)/shard_map/ppermute | solution.py:47
  18.6 3.8 %collective-permute-done.19 = f32[32,128]{1,0:T(8,128)S(1)} collective-permute-done((f32[32,128]{1,0:T(8,128)S(1)}, f32[32,128]{1,0:T(8,128)S(1)}, u32[]{:S(2)}, u32[]{:S(2)}) %collective-permute-start.19) | collective-permute-done | bytes 16416 | tf_op jit(solution)/shard_map/ppermute | solution.py:47
  22.5 7.4 %collective-permute-start.21 = (f32[128,128]{1,0:T(8,128)S(1)}, f32[128,128]{1,0:T(8,128)S(1)}, u32[]{:S(2)}, u32[]{:S(2)}) collective-permute-start(f32[128,128]{1,0:T(8,128)S(1)} %get-tuple-element.41), channel_id=1, source_target_pairs={{0,128},{1,129},{2,130},{3,131},{4,132},{5,133},{6,134},{7,135},{8... | collective-permute-start | bytes 196616 | tf_op jit(solution)/shard_map/ppermute | solution.py:47
  29.9 1.4 %collective-permute-start.3 = (f32[360,128]{1,0:T(8,128)S(1)}, f32[360,128]{1,0:T(8,128)S(1)}, u32[]{:S(2)}, u32[]{:S(2)}) collective-permute-start(f32[360,128]{1,0:T(8,128)S(1)} %get-tuple-element.27), channel_id=1, source_target_pairs={{0,8},{1,9},{2,10},{3,11},{4,12},{5,13},{6,14},{7,15},{8,0},{9,1},... | collective-permute-start | bytes 552968 | tf_op jit(solution)/shard_map/ppermute | solution.py:39
  33.1 3.0 %collective-permute-start.5 = (f32[360,128]{1,0:T(8,128)S(1)}, f32[360,128]{1,0:T(8,128)S(1)}, u32[]{:S(2)}, u32[]{:S(2)}) collective-permute-start(f32[360,128]{1,0:T(8,128)S(1)} %get-tuple-element.29), channel_id=1, source_target_pairs={{0,12},{1,13},{2,14},{3,15},{4,0},{5,1},{6,2},{7,3},{8,4},{9,5},{1... | collective-permute-start | bytes 552968 | tf_op jit(solution)/shard_map/ppermute | solution.py:39
  36.1 1.7 %collective-permute-start.6 = (f32[360,128]{1,0:T(8,128)S(1)}, f32[360,128]{1,0:T(8,128)S(1)}, u32[]{:S(2)}, u32[]{:S(2)}) collective-permute-start(f32[360,128]{1,0:T(8,128)S(1)} %get-tuple-element.30), channel_id=1, source_target_pairs={{0,14},{1,15},{2,12},{3,13},{4,2},{5,3},{6,0},{7,1},{8,6},{9,7},{1... | collective-permute-start | bytes 552968 | tf_op jit(solution)/shard_map/ppermute | solution.py:39
  39.0 2.8 %collective-permute-done.4.refs_5_ = f32[360,128]{1,0:T(8,128)S(1)} collective-permute-done((f32[360,128]{1,0:T(8,128)S(1)}, f32[360,128]{1,0:T(8,128)S(1)}, u32[]{:S(2)}, u32[]{:S(2)}) %collective-permute-start.4) | collective-permute-done | bytes 184352 | tf_op jit(solution)/shard_map/ppermute | solution.py:39
  41.8 1.2 %collective-permute-done.5.refs_6_ = f32[360,128]{1,0:T(8,128)S(1)} collective-permute-done((f32[360,128]{1,0:T(8,128)S(1)}, f32[360,128]{1,0:T(8,128)S(1)}, u32[]{:S(2)}, u32[]{:S(2)}) %collective-permute-start.5) | collective-permute-done | bytes 184352 | tf_op jit(solution)/shard_map/ppermute | solution.py:39
  43.0 1.5 %collective-permute-start.24 = (f32[256,128]{1,0:T(8,128)S(1)}, f32[256,128]{1,0:T(8,128)S(1)}, u32[]{:S(2)}, u32[]{:S(2)}) collective-permute-start(f32[256,128]{1,0:T(8,128)S(1)} %constant_dynamic-update-slice_fusion.11.refs_0_), channel_id=1, source_target_pairs={{0,64},{1,193},{2,66},{3,195},{4,68},{5,197},{6,70},{7,199},{8,72}... | collective-permute-start | bytes 393224 | tf_op jit(solution)/shard_map/ppermute | solution.py:47
  44.5 1.2 %collective-permute-done.6.refs_7_ = f32[360,128]{1,0:T(8,128)S(1)} collective-permute-done((f32[360,128]{1,0:T(8,128)S(1)}, f32[360,128]{1,0:T(8,128)S(1)}, u32[]{:S(2)}, u32[]{:S(2)}) %collective-permute-start.6) | collective-permute-done | bytes 184352 | tf_op jit(solution)/shard_map/ppermute | solution.py:39
  45.6 2.9 %collective-permute-start.23 = (f32[256,128]{1,0:T(8,128)S(1)}, f32[256,128]{1,0:T(8,128)S(1)}, u32[]{:S(2)}, u32[]{:S(2)}) collective-permute-start(f32[256,128]{1,0:T(8,128)S(1)} %constant_dynamic-update-slice_fusion.11.refs_0_), channel_id=1, source_target_pairs={{0,224},{1,225},{2,226},{3,227},{4,228},{5,229},{6,230},{7,231},{8... | collective-permute-start | bytes 393224 | tf_op jit(solution)/shard_map/ppermute | solution.py:47
  48.5 2.1 %collective-permute-done.24.refs_3_ = f32[256,128]{1,0:T(8,128)S(1)} collective-permute-done((f32[256,128]{1,0:T(8,128)S(1)}, f32[256,128]{1,0:T(8,128)S(1)}, u32[]{:S(2)}, u32[]{:S(2)}) %collective-permute-start.24) | collective-permute-done | bytes 131104 | tf_op jit(solution)/shard_map/ppermute | solution.py:47
  50.5 1.5 %collective-permute-done.23.refs_2_ = f32[256,128]{1,0:T(8,128)S(1)} collective-permute-done((f32[256,128]{1,0:T(8,128)S(1)}, f32[256,128]{1,0:T(8,128)S(1)}, u32[]{:S(2)}, u32[]{:S(2)}) %collective-permute-start.23) | collective-permute-done | bytes 131104 | tf_op jit(solution)/shard_map/ppermute | solution.py:47
  52.4 2.3 %collective-permute-done.22.refs_1_ = f32[256,128]{1,0:T(8,128)S(1)} collective-permute-done((f32[256,128]{1,0:T(8,128)S(1)}, f32[256,128]{1,0:T(8,128)S(1)}, u32[]{:S(2)}, u32[]{:S(2)}) %collective-permute-start.22) | collective-permute-done | bytes 131104 | tf_op jit(solution)/shard_map/ppermute | solution.py:47
  56.6 2.1 %shard_map.39 = (f32[360,128]{1,0:T(8,128)S(1)}, f32[360,128]{1,0:T(8,128)S(1)}, f32[360,128]{1,0:T(8,128)S(1)}, f32[360,128]{1,0:T(8,128)S(1)}, f32[360,128]{1,...) custom-call(f32[360,128]{1,0:T(8,128)S(1)} %get-tuple-element.23.refs_0_, ...), custom_call_target="tpu_custom_call" | custom-call | flops 1132462080 | bytes 4947968 | tf_op jit(solution)/shard_map/pallas_call | solution.py:164
  58.7 1.8 %collective-permute-start.25 = (f32[360,128]{1,0:T(8,128)S(1)}, f32[360,128]{1,0:T(8,128)S(1)}, u32[]{:S(2)}, u32[]{:S(2)}) collective-permute-start(f32[360,128]{1,0:T(8,128)S(1)} %get-tuple-element.34), channel_id=1, source_target_pairs={{0,2},{1,3},{2,0},{3,1},{4,6},{5,7},{6,4},{7,5},{8,10},{9,11},{10,... | collective-permute-start | bytes 552968 | tf_op jit(solution)/shard_map/ppermute | solution.py:39
  61.2 1.1 %collective-permute-start.27 = (f32[360,128]{1,0:T(8,128)S(1)}, f32[360,128]{1,0:T(8,128)S(1)}, u32[]{:S(2)}, u32[]{:S(2)}) collective-permute-start(f32[360,128]{1,0:T(8,128)S(1)} %get-tuple-element.36), channel_id=1, source_target_pairs={{0,6},{1,7},{2,4},{3,5},{4,10},{5,11},{6,8},{7,9},{8,14},{9,15},{1... | collective-permute-start | bytes 552968 | tf_op jit(solution)/shard_map/ppermute | solution.py:39
  62.3 2.1 %collective-permute-start.28 = (f32[360,128]{1,0:T(8,128)S(1)}, f32[360,128]{1,0:T(8,128)S(1)}, u32[]{:S(2)}, u32[]{:S(2)}) collective-permute-start(f32[360,128]{1,0:T(8,128)S(1)} %get-tuple-element.37), channel_id=1, source_target_pairs={{0,8},{1,9},{2,10},{3,11},{4,12},{5,13},{6,14},{7,15},{8,0},{9,1},... | collective-permute-start | bytes 552968 | tf_op jit(solution)/shard_map/ppermute | solution.py:39
  64.4 2.6 %collective-permute-start.29 = (f32[360,128]{1,0:T(8,128)S(1)}, f32[360,128]{1,0:T(8,128)S(1)}, u32[]{:S(2)}, u32[]{:S(2)}) collective-permute-start(f32[360,128]{1,0:T(8,128)S(1)} %get-tuple-element.38), channel_id=1, source_target_pairs={{0,10},{1,11},{2,8},{3,9},{4,14},{5,15},{6,12},{7,13},{8,2},{9,3},... | collective-permute-start | bytes 552968 | tf_op jit(solution)/shard_map/ppermute | solution.py:39
  68.1 1.9 %collective-permute-start.31 = (f32[360,128]{1,0:T(8,128)S(1)}, f32[360,128]{1,0:T(8,128)S(1)}, u32[]{:S(2)}, u32[]{:S(2)}) collective-permute-start(f32[360,128]{1,0:T(8,128)S(1)} %get-tuple-element.40), channel_id=1, source_target_pairs={{0,14},{1,15},{2,12},{3,13},{4,2},{5,3},{6,0},{7,1},{8,6},{9,7},{1... | collective-permute-start | bytes 552968 | tf_op jit(solution)/shard_map/ppermute | solution.py:39
  70.0 2.0 %collective-permute-done.27.refs_3_ = f32[360,128]{1,0:T(8,128)S(1)} collective-permute-done((f32[360,128]{1,0:T(8,128)S(1)}, f32[360,128]{1,0:T(8,128)S(1)}, u32[]{:S(2)}, u32[]{:S(2)}) %collective-permute-start.27) | collective-permute-done | bytes 184352 | tf_op jit(solution)/shard_map/ppermute | solution.py:39
  72.0 4.5 %collective-permute-done.29.refs_5_ = f32[360,128]{1,0:T(8,128)S(1)} collective-permute-done((f32[360,128]{1,0:T(8,128)S(1)}, f32[360,128]{1,0:T(8,128)S(1)}, u32[]{:S(2)}, u32[]{:S(2)}) %collective-permute-start.29) | collective-permute-done | bytes 184352 | tf_op jit(solution)/shard_map/ppermute | solution.py:39
  76.5 1.3 %collective-permute-done.30.refs_6_ = f32[360,128]{1,0:T(8,128)S(1)} collective-permute-done((f32[360,128]{1,0:T(8,128)S(1)}, f32[360,128]{1,0:T(8,128)S(1)}, u32[]{:S(2)}, u32[]{:S(2)}) %collective-permute-start.30) | collective-permute-done | bytes 184352 | tf_op jit(solution)/shard_map/ppermute | solution.py:39
  77.8 4.9 %collective-permute-done.31.refs_7_ = f32[360,128]{1,0:T(8,128)S(1)} collective-permute-done((f32[360,128]{1,0:T(8,128)S(1)}, f32[360,128]{1,0:T(8,128)S(1)}, u32[]{:S(2)}, u32[]{:S(2)}) %collective-permute-start.31) | collective-permute-done | bytes 184352 | tf_op jit(solution)/shard_map/ppermute | solution.py:39
  82.7 1.4 %shard_map.40 = f32[32,11520]{1,0:T(8,128)} custom-call(f32[360,128]{1,0:T(8,128)S(1)} %get-tuple-element.33.refs_0_, f32[360,128]{1,0:T(8,128)S(1)} %collective-permute-done.25.refs_1_, f32[360,128]{1,0:T(8,128)S(1)} %collective-permute-done.26.refs_2_, f32[360,128]{1,0:T(8,128)S(1)} %collective-permute-done.27.refs_3_, ...), custom_call_target="tpu_custom_call" | custom-call | bytes 4423680 | tf_op jit(solution)/shard_map/pallas_call | solution.py:164
  (49 shorter events, 9.7 us)
Async XLA Ops:
  0.7 8.5 %collective-permute-start.17 = (f32[8,128]{1,0:T(8,128)S(1)}, f32[8,128]{1,0:T(8,128)S(1)}, u32[]{:S(2)}, u32[]{:S(2)}) collective-permute-start(f32[8,128]{1,0:T(8,128)S(1)} %reshape.3), channel_id=1, source_target_pairs={{0,18},{1,19},{2,0},{3,1},{4,22},{5,23},{6,4},{7,5},{8,26},{9,27},... | collective-permute-start | bytes 12296 | tf_op jit(solution)/shard_map/ppermute | solution.py:47
  3.7 5.5 %collective-permute-start.16 = (f32[8,128]{1,0:T(8,128)S(1)}, f32[8,128]{1,0:T(8,128)S(1)}, u32[]{:S(2)}, u32[]{:S(2)}) collective-permute-start(f32[8,128]{1,0:T(8,128)S(1)} %reshape.3), channel_id=1, source_target_pairs={{0,16},{1,17},{2,18},{3,19},{4,20},{5,21},{6,22},{7,23},{8,24},{9,... | collective-permute-start | bytes 12296 | tf_op jit(solution)/shard_map/ppermute | solution.py:47
  4.3 4.8 %collective-permute-start.15 = (f32[8,128]{1,0:T(8,128)S(1)}, f32[8,128]{1,0:T(8,128)S(1)}, u32[]{:S(2)}, u32[]{:S(2)}) collective-permute-start(f32[8,128]{1,0:T(8,128)S(1)} %reshape.3), channel_id=1, source_target_pairs={{0,2},{1,3},{2,16},{3,17},{4,6},{5,7},{6,20},{7,21},{8,10},{9,11},... | collective-permute-start | bytes 12296 | tf_op jit(solution)/shard_map/ppermute | solution.py:47
  9.2 8.0 %collective-permute-start.18 = (f32[32,128]{1,0:T(8,128)S(1)}, f32[32,128]{1,0:T(8,128)S(1)}, u32[]{:S(2)}, u32[]{:S(2)}) collective-permute-start(f32[32,128]{1,0:T(8,128)S(1)} %get-tuple-element.49), channel_id=1, source_target_pairs={{0,4},{1,5},{2,6},{3,7},{4,8},{5,9},{6,10},{7,11},{8,12},{9,13},{1... | collective-permute-start | bytes 49160 | tf_op jit(solution)/shard_map/ppermute | solution.py:47
  12.4 20.7 %collective-permute-start = (f32[360,128]{1,0:T(8,128)S(1)}, f32[360,128]{1,0:T(8,128)S(1)}, u32[]{:S(2)}, u32[]{:S(2)}) collective-permute-start(f32[360,128]{1,0:T(8,128)S(1)} %get-tuple-element.24), channel_id=1, source_target_pairs={{0,2},{1,3},{2,0},{3,1},{4,6},{5,7},{6,4},{7,5},{8,10},{9,11},{10,... | collective-permute-start | bytes 552968 | tf_op jit(solution)/shard_map/ppermute | solution.py:39
  12.5 23.6 %collective-permute-start.1 = (f32[360,128]{1,0:T(8,128)S(1)}, f32[360,128]{1,0:T(8,128)S(1)}, u32[]{:S(2)}, u32[]{:S(2)}) collective-permute-start(f32[360,128]{1,0:T(8,128)S(1)} %get-tuple-element.25), channel_id=1, source_target_pairs={{0,4},{1,5},{2,6},{3,7},{4,8},{5,9},{6,10},{7,11},{8,12},{9,13},{1... | collective-permute-start | bytes 552968 | tf_op jit(solution)/shard_map/ppermute | solution.py:39
  13.8 24.0 %collective-permute-start.2 = (f32[360,128]{1,0:T(8,128)S(1)}, f32[360,128]{1,0:T(8,128)S(1)}, u32[]{:S(2)}, u32[]{:S(2)}) collective-permute-start(f32[360,128]{1,0:T(8,128)S(1)} %get-tuple-element.26), channel_id=1, source_target_pairs={{0,6},{1,7},{2,4},{3,5},{4,10},{5,11},{6,8},{7,9},{8,14},{9,15},{1... | collective-permute-start | bytes 552968 | tf_op jit(solution)/shard_map/ppermute | solution.py:39
  15.7 6.8 %collective-permute-start.20 = (f32[32,128]{1,0:T(8,128)S(1)}, f32[32,128]{1,0:T(8,128)S(1)}, u32[]{:S(2)}, u32[]{:S(2)}) collective-permute-start(f32[32,128]{1,0:T(8,128)S(1)} %get-tuple-element.49), channel_id=1, source_target_pairs={{0,12},{1,13},{2,14},{3,15},{4,0},{5,1},{6,2},{7,3},{8,4},{9,5},{1... | collective-permute-start | bytes 49160 | tf_op jit(solution)/shard_map/ppermute | solution.py:47
  17.2 5.2 %collective-permute-start.19 = (f32[32,128]{1,0:T(8,128)S(1)}, f32[32,128]{1,0:T(8,128)S(1)}, u32[]{:S(2)}, u32[]{:S(2)}) collective-permute-start(f32[32,128]{1,0:T(8,128)S(1)} %get-tuple-element.49), channel_id=1, source_target_pairs={{0,8},{1,9},{2,10},{3,11},{4,12},{5,13},{6,14},{7,15},{8,0},{9,1},... | collective-permute-start | bytes 49160 | tf_op jit(solution)/shard_map/ppermute | solution.py:47
  22.5 9.7 %collective-permute-start.21 = (f32[128,128]{1,0:T(8,128)S(1)}, f32[128,128]{1,0:T(8,128)S(1)}, u32[]{:S(2)}, u32[]{:S(2)}) collective-permute-start(f32[128,128]{1,0:T(8,128)S(1)} %get-tuple-element.41), channel_id=1, source_target_pairs={{0,128},{1,129},{2,130},{3,131},{4,132},{5,133},{6,134},{7,135},{8... | collective-permute-start | bytes 196616 | tf_op jit(solution)/shard_map/ppermute | solution.py:47
  29.9 9.1 %collective-permute-start.3 = (f32[360,128]{1,0:T(8,128)S(1)}, f32[360,128]{1,0:T(8,128)S(1)}, u32[]{:S(2)}, u32[]{:S(2)}) collective-permute-start(f32[360,128]{1,0:T(8,128)S(1)} %get-tuple-element.27), channel_id=1, source_target_pairs={{0,8},{1,9},{2,10},{3,11},{4,12},{5,13},{6,14},{7,15},{8,0},{9,1},... | collective-permute-start | bytes 552968 | tf_op jit(solution)/shard_map/ppermute | solution.py:39
  32.2 9.5 %collective-permute-start.4 = (f32[360,128]{1,0:T(8,128)S(1)}, f32[360,128]{1,0:T(8,128)S(1)}, u32[]{:S(2)}, u32[]{:S(2)}) collective-permute-start(f32[360,128]{1,0:T(8,128)S(1)} %get-tuple-element.28), channel_id=1, source_target_pairs={{0,10},{1,11},{2,8},{3,9},{4,14},{5,15},{6,12},{7,13},{8,2},{9,3},... | collective-permute-start | bytes 552968 | tf_op jit(solution)/shard_map/ppermute | solution.py:39
  33.1 9.9 %collective-permute-start.5 = (f32[360,128]{1,0:T(8,128)S(1)}, f32[360,128]{1,0:T(8,128)S(1)}, u32[]{:S(2)}, u32[]{:S(2)}) collective-permute-start(f32[360,128]{1,0:T(8,128)S(1)} %get-tuple-element.29), channel_id=1, source_target_pairs={{0,12},{1,13},{2,14},{3,15},{4,0},{5,1},{6,2},{7,3},{8,4},{9,5},{1... | collective-permute-start | bytes 552968 | tf_op jit(solution)/shard_map/ppermute | solution.py:39
  36.1 9.5 %collective-permute-start.6 = (f32[360,128]{1,0:T(8,128)S(1)}, f32[360,128]{1,0:T(8,128)S(1)}, u32[]{:S(2)}, u32[]{:S(2)}) collective-permute-start(f32[360,128]{1,0:T(8,128)S(1)} %get-tuple-element.30), channel_id=1, source_target_pairs={{0,14},{1,15},{2,12},{3,13},{4,2},{5,3},{6,0},{7,1},{8,6},{9,7},{1... | collective-permute-start | bytes 552968 | tf_op jit(solution)/shard_map/ppermute | solution.py:39
  37.8 10.6 %collective-permute-start.7 = (f32[360,128]{1,0:T(8,128)S(1)}, f32[360,128]{1,0:T(8,128)S(1)}, u32[]{:S(2)}, u32[]{:S(2)}) collective-permute-start(f32[360,128]{1,0:T(8,128)S(1)} %get-tuple-element.23.refs_0_), channel_id=1, source_target_pairs={{0,1},{1,0},{2,3},{3,2},{4,5},{5,4},{6,7},{7,6},{8,9},{9,8},{10,11... | collective-permute-start | bytes 552968 | tf_op jit(solution)/shard_map/ppermute | solution.py:43
  39.0 15.7 %collective-permute-start.8 = (f32[360,128]{1,0:T(8,128)S(1)}, f32[360,128]{1,0:T(8,128)S(1)}, u32[]{:S(2)}, u32[]{:S(2)}) collective-permute-start(f32[360,128]{1,0:T(8,128)S(1)} %collective-permute-done.refs_1_), channel_id=1, source_target_pairs={{0,1},{1,0},{2,3},{3,2},{4,5},{5,4},{6,7},{7,6},{8,9},{9,8},{10,11... | collective-permute-start | bytes 552968 | tf_op jit(solution)/shard_map/ppermute | solution.py:43
  41.8 13.4 %collective-permute-start.9 = (f32[360,128]{1,0:T(8,128)S(1)}, f32[360,128]{1,0:T(8,128)S(1)}, u32[]{:S(2)}, u32[]{:S(2)}) collective-permute-start(f32[360,128]{1,0:T(8,128)S(1)} %collective-permute-done.1.refs_2_), channel_id=1, source_target_pairs={{0,1},{1,0},{2,3},{3,2},{4,5},{5,4},{6,7},{7,6},{8,9},{9,8},{10,11... | collective-permute-start | bytes 552968 | tf_op jit(solution)/shard_map/ppermute | solution.py:43
  43.0 7.6 %collective-permute-start.24 = (f32[256,128]{1,0:T(8,128)S(1)}, f32[256,128]{1,0:T(8,128)S(1)}, u32[]{:S(2)}, u32[]{:S(2)}) collective-permute-start(f32[256,128]{1,0:T(8,128)S(1)} %constant_dynamic-update-slice_fusion.11.refs_0_), channel_id=1, source_target_pairs={{0,64},{1,193},{2,66},{3,195},{4,68},{5,197},{6,70},{7,199},{8,72}... | collective-permute-start | bytes 393224 | tf_op jit(solution)/shard_map/ppermute | solution.py:47
  45.6 6.4 %collective-permute-start.23 = (f32[256,128]{1,0:T(8,128)S(1)}, f32[256,128]{1,0:T(8,128)S(1)}, u32[]{:S(2)}, u32[]{:S(2)}) collective-permute-start(f32[256,128]{1,0:T(8,128)S(1)} %constant_dynamic-update-slice_fusion.11.refs_0_), channel_id=1, source_target_pairs={{0,224},{1,225},{2,226},{3,227},{4,228},{5,229},{6,230},{7,231},{8... | collective-permute-start | bytes 393224 | tf_op jit(solution)/shard_map/ppermute | solution.py:47
  48.5 6.2 %collective-permute-start.22 = (f32[256,128]{1,0:T(8,128)S(1)}, f32[256,128]{1,0:T(8,128)S(1)}, u32[]{:S(2)}, u32[]{:S(2)}) collective-permute-start(f32[256,128]{1,0:T(8,128)S(1)} %constant_dynamic-update-slice_fusion.11.refs_0_), channel_id=1, source_target_pairs={{0,32},{1,33},{2,34},{3,35},{4,36},{5,37},{6,38},{7,39},{8,40},{9,... | collective-permute-start | bytes 393224 | tf_op jit(solution)/shard_map/ppermute | solution.py:47
  50.5 5.2 %collective-permute-start.10 = (f32[360,128]{1,0:T(8,128)S(1)}, f32[360,128]{1,0:T(8,128)S(1)}, u32[]{:S(2)}, u32[]{:S(2)}) collective-permute-start(f32[360,128]{1,0:T(8,128)S(1)} %collective-permute-done.2.refs_3_), channel_id=1, source_target_pairs={{0,1},{1,0},{2,3},{3,2},{4,5},{5,4},{6,7},{7,6},{8,9},{9,8},{10,11... | collective-permute-start | bytes 552968 | tf_op jit(solution)/shard_map/ppermute | solution.py:43
  52.0 3.7 %collective-permute-start.11 = (f32[360,128]{1,0:T(8,128)S(1)}, f32[360,128]{1,0:T(8,128)S(1)}, u32[]{:S(2)}, u32[]{:S(2)}) collective-permute-start(f32[360,128]{1,0:T(8,128)S(1)} %collective-permute-done.3.refs_4_), channel_id=1, source_target_pairs={{0,1},{1,0},{2,3},{3,2},{4,5},{5,4},{6,7},{7,6},{8,9},{9,8},{10,11... | collective-permute-start | bytes 552968 | tf_op jit(solution)/shard_map/ppermute | solution.py:43
  54.7 1.4 %collective-permute-start.12 = (f32[360,128]{1,0:T(8,128)S(1)}, f32[360,128]{1,0:T(8,128)S(1)}, u32[]{:S(2)}, u32[]{:S(2)}) collective-permute-start(f32[360,128]{1,0:T(8,128)S(1)} %collective-permute-done.4.refs_5_), channel_id=1, source_target_pairs={{0,1},{1,0},{2,3},{3,2},{4,5},{5,4},{6,7},{7,6},{8,9},{9,8},{10,11... | collective-permute-start | bytes 552968 | tf_op jit(solution)/shard_map/ppermute | solution.py:43
  54.7 1.7 %collective-permute-start.13 = (f32[360,128]{1,0:T(8,128)S(1)}, f32[360,128]{1,0:T(8,128)S(1)}, u32[]{:S(2)}, u32[]{:S(2)}) collective-permute-start(f32[360,128]{1,0:T(8,128)S(1)} %collective-permute-done.5.refs_6_), channel_id=1, source_target_pairs={{0,1},{1,0},{2,3},{3,2},{4,5},{5,4},{6,7},{7,6},{8,9},{9,8},{10,11... | collective-permute-start | bytes 552968 | tf_op jit(solution)/shard_map/ppermute | solution.py:43
  55.2 1.4 %collective-permute-start.14 = (f32[360,128]{1,0:T(8,128)S(1)}, f32[360,128]{1,0:T(8,128)S(1)}, u32[]{:S(2)}, u32[]{:S(2)}) collective-permute-start(f32[360,128]{1,0:T(8,128)S(1)} %collective-permute-done.6.refs_7_), channel_id=1, source_target_pairs={{0,1},{1,0},{2,3},{3,2},{4,5},{5,4},{6,7},{7,6},{8,9},{9,8},{10,11... | collective-permute-start | bytes 552968 | tf_op jit(solution)/shard_map/ppermute | solution.py:43
  58.7 8.2 %collective-permute-start.25 = (f32[360,128]{1,0:T(8,128)S(1)}, f32[360,128]{1,0:T(8,128)S(1)}, u32[]{:S(2)}, u32[]{:S(2)}) collective-permute-start(f32[360,128]{1,0:T(8,128)S(1)} %get-tuple-element.34), channel_id=1, source_target_pairs={{0,2},{1,3},{2,0},{3,1},{4,6},{5,7},{6,4},{7,5},{8,10},{9,11},{10,... | collective-permute-start | bytes 552968 | tf_op jit(solution)/shard_map/ppermute | solution.py:39
  60.6 7.5 %collective-permute-start.26 = (f32[360,128]{1,0:T(8,128)S(1)}, f32[360,128]{1,0:T(8,128)S(1)}, u32[]{:S(2)}, u32[]{:S(2)}) collective-permute-start(f32[360,128]{1,0:T(8,128)S(1)} %get-tuple-element.35), channel_id=1, source_target_pairs={{0,4},{1,5},{2,6},{3,7},{4,8},{5,9},{6,10},{7,11},{8,12},{9,13},{1... | collective-permute-start | bytes 552968 | tf_op jit(solution)/shard_map/ppermute | solution.py:39
  61.2 10.9 %collective-permute-start.27 = (f32[360,128]{1,0:T(8,128)S(1)}, f32[360,128]{1,0:T(8,128)S(1)}, u32[]{:S(2)}, u32[]{:S(2)}) collective-permute-start(f32[360,128]{1,0:T(8,128)S(1)} %get-tuple-element.36), channel_id=1, source_target_pairs={{0,6},{1,7},{2,4},{3,5},{4,10},{5,11},{6,8},{7,9},{8,14},{9,15},{1... | collective-permute-start | bytes 552968 | tf_op jit(solution)/shard_map/ppermute | solution.py:39
  62.3 9.7 %collective-permute-start.28 = (f32[360,128]{1,0:T(8,128)S(1)}, f32[360,128]{1,0:T(8,128)S(1)}, u32[]{:S(2)}, u32[]{:S(2)}) collective-permute-start(f32[360,128]{1,0:T(8,128)S(1)} %get-tuple-element.37), channel_id=1, source_target_pairs={{0,8},{1,9},{2,10},{3,11},{4,12},{5,13},{6,14},{7,15},{8,0},{9,1},... | collective-permute-start | bytes 552968 | tf_op jit(solution)/shard_map/ppermute | solution.py:39
  64.4 12.1 %collective-permute-start.29 = (f32[360,128]{1,0:T(8,128)S(1)}, f32[360,128]{1,0:T(8,128)S(1)}, u32[]{:S(2)}, u32[]{:S(2)}) collective-permute-start(f32[360,128]{1,0:T(8,128)S(1)} %get-tuple-element.38), channel_id=1, source_target_pairs={{0,10},{1,11},{2,8},{3,9},{4,14},{5,15},{6,12},{7,13},{8,2},{9,3},... | collective-permute-start | bytes 552968 | tf_op jit(solution)/shard_map/ppermute | solution.py:39
  67.0 10.8 %collective-permute-start.30 = (f32[360,128]{1,0:T(8,128)S(1)}, f32[360,128]{1,0:T(8,128)S(1)}, u32[]{:S(2)}, u32[]{:S(2)}) collective-permute-start(f32[360,128]{1,0:T(8,128)S(1)} %get-tuple-element.39), channel_id=1, source_target_pairs={{0,12},{1,13},{2,14},{3,15},{4,0},{5,1},{6,2},{7,3},{8,4},{9,5},{1... | collective-permute-start | bytes 552968 | tf_op jit(solution)/shard_map/ppermute | solution.py:39
  68.1 14.7 %collective-permute-start.31 = (f32[360,128]{1,0:T(8,128)S(1)}, f32[360,128]{1,0:T(8,128)S(1)}, u32[]{:S(2)}, u32[]{:S(2)}) collective-permute-start(f32[360,128]{1,0:T(8,128)S(1)} %get-tuple-element.40), channel_id=1, source_target_pairs={{0,14},{1,15},{2,12},{3,13},{4,2},{5,3},{6,0},{7,1},{8,6},{9,7},{1... | collective-permute-start | bytes 552968 | tf_op jit(solution)/shard_map/ppermute | solution.py:39
  (2 other events, 27.5 us)

commit v2 on v0

v2 whole, which is shorter than its diff:
```python
import functools

import jax
import jax.numpy as jnp
from jax import lax
from jax.experimental import pallas as pl
from jax.experimental.pallas import tpu as pltpu
from jax.sharding import PartitionSpec as P

LANES = 128
ROWS = 32
TILES = 11
SPLIT = 8 * TILES * LANES
MSG = TILES * ROWS + 8
MIB = 1 << 20
OVER_CHIPS = [[c for c in range(16) if c % 2 == k] for k in range(2)]
OFFSETS = [(dx, dy) for dx in range(4) for dy in range(2)]


def cols(f):
    pairs = []
    for c in range(16):
        x, y, k = f(c >> 2, (c >> 1) & 1, c & 1)
        pairs.append((c, 4 * (x % 4) + 2 * (y % 2) + k % 2))
    return pairs


def rows(f):
    pairs = []
    for d in range(256):
        r, c = d >> 4, d & 15
        z, y = f(r >> 1, r & 1, c & 1)
        pairs.append((d, 16 * (2 * (z % 8) + y % 2) + c))
    return pairs


def over_chips(a):
    return lax.all_to_all(a, "col", 0, 0, tiled=True, axis_index_groups=OVER_CHIPS)


def to_chip(a, dx, dy):
    return lax.ppermute(a, "col", cols(lambda x, y, k: (x + dx, y + dy, k)))


def swap_cores(a):
    return lax.ppermute(a, "col", cols(lambda x, y, k: (x, y, k + 1)))


def over_rows(a, f):
    return lax.ppermute(a, ("row", "col"), rows(f))


def here():
    col, row = lax.axis_index("col"), lax.axis_index("row")
    return col // 4, (col // 2) % 2, col % 2, row


def split(a):
    hi = a.astype(jnp.bfloat16)
    return hi, (a - hi.astype(jnp.float32)).astype(jnp.bfloat16)


def lane_group():
    return lax.broadcasted_iota(jnp.int32, (8, LANES), 1) // ROWS


def pack_kernel(v, msgs):
    for q in range(8):
        for t in range(TILES):
            at = (q * TILES + t) * LANES
            msgs[q, t * ROWS : (t + 1) * ROWS, :] = v[:, at : at + LANES]
        at = SPLIT + q // 4 * LANES
        folded = v[:8, at : at + LANES]
        for g in range(4):
            part = pltpu.roll(v[8 * g : 8 * g + 8, at : at + LANES], (ROWS * (g + 4 - q % 4)) % LANES, 1)
            folded = jnp.where(lane_group() == g, part, folded)
        msgs[q, TILES * ROWS :, :] = folded


def tile_kernel(a, out):
    out[...] = jnp.concatenate([a[i : i + 1, c * LANES : (c + 1) * LANES] for i in range(2) for c in range(4)], axis=0)


def join_kernel(a, b, out):
    n = a.shape[0]
    out[:n, :] = a[...]
    out[n:, :] = b[...]


def collect_kernel(*refs):
    parts, out = refs[:4], refs[4]
    _, _, k, row = here()
    for jz, part in enumerate(parts):
        back = (0, 1, 7, 2 + 4 * k)[jz]
        for j4 in range(2):
            for jy in range(2):
                r = 2 * ((row // 2 + 16 - back - 4 * j4) % 8) + (row + jy) % 2
                j = 2 * j4 + jy
                out[pl.ds(pl.multiple_of(8 * r, 8), 8), :] = part[8 * j : 8 * j + 8, :]


def unpack(msg, v_hi, v_lo, at):
    at = pl.ds(pl.multiple_of(at, ROWS), ROWS)
    for t in range(TILES):
        hi, lo = split(msg[t * ROWS : (t + 1) * ROWS, :])
        v_hi[at, t * LANES : (t + 1) * LANES] = hi
        v_lo[at, t * LANES : (t + 1) * LANES] = lo
    folded = msg[TILES * ROWS :, :]
    rows = [folded] + [pltpu.roll(folded, LANES - ROWS * g, 1) for g in range(1, 4)]
    hi, lo = split(jnp.concatenate(rows, axis=0))
    v_hi[at, TILES * LANES :] = hi
    v_lo[at, TILES * LANES :] = lo


def ladder(t_hi, t_lo, v_hi, v_lo, msgs):
    dot = functools.partial(jnp.dot, preferred_element_type=jnp.float32)
    for j in range(6):
        lanes = slice(2 * j * LANES, (2 * j + 2) * LANES)
        hi, lo = v_hi[:, lanes], v_lo[:, lanes]
        out = dot(t_hi, hi) + (dot(t_hi, lo) + dot(t_lo, hi))
        for q, msg in enumerate(msgs):
            rows = out[q * ROWS : (q + 1) * ROWS]
            msg[2 * j * ROWS : (2 * j + 1) * ROWS, :] = rows[:, :LANES]
            if j < 5:
                msg[(2 * j + 1) * ROWS : (2 * j + 2) * ROWS, :] = rows[:, LANES:]
            else:
                folded = rows[:8, LANES:]
                for g in range(1, 4):
                    part = pltpu.roll(rows[8 * g : 8 * g + 8, LANES:], ROWS * g, 1)
                    folded = jnp.where(lane_group() == g, part, folded)
                msg[TILES * ROWS :, :] = folded


def amplitude_rows(amps):
    his, los = [], []
    for amp in amps:
        parts = [split(amp[pl.ds(c, ROWS, stride=4), :]) for c in range(4)]
        his.append(jnp.concatenate([p[0] for p in parts], axis=1))
        los.append(jnp.concatenate([p[1] for p in parts], axis=1))
    return jnp.concatenate(his, axis=0), jnp.concatenate(los, axis=0)


def first_kernel(n, mine, other, *refs):
    amps, msgs, (v_hi, v_lo) = refs[:n], refs[n : 2 * n], refs[2 * n :]
    _, _, k, _ = here()
    for q in range(8):
        unpack(mine.at[q], v_hi, v_lo, (2 * q + k) * ROWS)
        unpack(other.at[q], v_hi, v_lo, (2 * q + 1 - k) * ROWS)
    ladder(*amplitude_rows(amps), v_hi, v_lo, msgs)


def later_kernel(n, v_hi, v_lo, *refs):
    ladder(*amplitude_rows(refs[:n]), v_hi, v_lo, refs[n:])


def chip(o, sign, relative):
    if not relative:
        return o
    x, y, _, _ = here()
    dx, dy = OFFSETS[o]
    return 2 * ((x + 4 + sign * dx) % 4) + (y + dy) % 2


def add_rel_kernel(*refs):
    msgs, previous, out = refs[:8], refs[8], refs[9]
    group = lane_group()
    narrow = [[jnp.zeros((8, LANES), jnp.float32) for _ in range(4)] for _ in range(2)]
    for o in range(8):
        q = chip(o, -1, True)
        for t in range(TILES):
            at = pl.ds(pl.multiple_of((q * TILES + t) * LANES, LANES), LANES)
            out[:, at] = previous[:, at] + msgs[o][t * ROWS : (t + 1) * ROWS, :]
        folded = msgs[o][TILES * ROWS :, :]
        for g in range(4):
            part = pltpu.roll(folded, (ROWS * (q % 4 + 4 - g)) % LANES, 1)
            for j in range(2):
                narrow[j][g] = jnp.where(group + 4 * j == q, part, narrow[j][g])
    for j in range(2):
        at = slice(SPLIT + j * LANES, SPLIT + (j + 1) * LANES)
        out[:, at] = previous[:, at] + jnp.concatenate(narrow[j], axis=0)


def call(kernel, outs, args, flops=0, scratch=(), limit=16):
    moved = sum(a.size * a.dtype.itemsize for a in list(args) + list(outs))
    return pl.pallas_call(
        kernel,
        out_shape=outs,
        in_specs=[pl.BlockSpec(memory_space=pltpu.VMEM)] * len(args),
        out_specs=jax.tree.map(lambda _: pl.BlockSpec(memory_space=pltpu.VMEM), outs),
        scratch_shapes=list(scratch),
        compiler_params=pltpu.CompilerParams(vmem_limit_bytes=limit * MIB),
        cost_estimate=pl.CostEstimate(flops=flops, bytes_accessed=moved, transcendentals=0),
    )(*args)


def f32(*shape):
    return jax.ShapeDtypeStruct(shape, jnp.float32)


GROUPS = [[(0, 0), (0, 1)], [(1, 0), (1, 1), (3, 0), (3, 1)], [(2, 0), (2, 1)]]


def body(amplitudes, integrals, previous):
    msg, stack = f32(MSG, LANES), f32(8, MSG, LANES)
    tile = call(tile_kernel, [f32(8, LANES)], [amplitudes])[0]
    part = call(join_kernel, [f32(16, LANES)], [tile, over_rows(tile, lambda z, y, k: (z, y + 1))])[0]
    sent = call(pack_kernel, [stack], [integrals])[0]
    sent, part = lax.optimization_barrier((sent, part))
    part = call(join_kernel, [f32(32, LANES)], [part, over_rows(part, lambda z, y, k: (z + 4, y))])[0]
    parts = [
        part,
        over_rows(part, lambda z, y, k: (z + 1, y)),
        over_rows(part, lambda z, y, k: (z - 1, y)),
        over_rows(part, lambda z, y, k: (z + 2 - 4 * k, y)),
    ]
    own = call(collect_kernel, [f32(128, LANES)], parts)[0]
    mine, _ = lax.optimization_barrier((over_chips(sent), own))
    amps = {o: to_chip(own, *o) for o in [(0, 1), (1, 0), (3, 0), (1, 1), (3, 1), (2, 0), (2, 1)]}
    amps[(0, 0)] = own
    other = swap_cores(mine)
    flops = 3 * 2 * 32 * 512 * 1440
    v_shape = jax.ShapeDtypeStruct((512, 12 * LANES), jnp.bfloat16)
    back = {}
    for i, group in enumerate(GROUPS):
        n = len(group)
        rows = [amps[o] for o in group]
        if i == 0:
            kernel, outs, args = first_kernel, [msg] * n + [v_shape] * 2, [mine, other] + rows
        else:
            if i == 2:
                *v, back[(0, 1)] = lax.optimization_barrier((*v, back[(0, 1)]))
            kernel, outs, args = later_kernel, [msg] * n, v + rows
        out = call(functools.partial(kernel, n), outs, args, n * flops, limit=32)
        v = list(out[n:]) if i == 0 else v
        for (dx, dy), m in zip(group, out):
            o = ((4 - dx) % 4, dy)
            back[o] = m if o == (0, 0) else to_chip(m, *o)
    return call(add_rel_kernel, [f32(*previous.shape)], [back[o] for o in OFFSETS] + [previous])[0]


def solution(mesh):
    in_specs = (P(("col", "row"), None), P("col", "row"), P("col", "row"))
    out_specs = P("col", "row")
    return jax.shard_map(body, mesh=mesh, in_specs=in_specs, out_specs=out_specs, check_vma=False)
```

time: 171 us -> 70.8 us (0.41)
  the two profiles are of different devices: /device:TPU:1 before, /device:TPU:2 now
where the time goes in v2:
time: 70.8 us; the launch traced here: 70.6 us
  starting transfers between devices  44.2 us (62%)
  waiting for transfers between devices  18.1 us (26%)
  Pallas kernels  6.17 us (9%)
  local copies, waits for them, and re-layouts  2.06 us (3%)
    ppermute x14, starting transfers between devices, to_chip(): return lax.ppermute(a, 'col', cols(lambda x, y, k: (x + dx, y + dy, k)))  23.9 us
    ppermute x5, starting transfers between devices, over_rows(): return lax.ppermute(a, ('row', 'col'), rows(f))  15 us
    ppermute x14, waiting for transfers between devices, to_chip(): return lax.ppermute(a, 'col', cols(lambda x, y, k: (x + dx, y + dy, k)))  10.6 us
    ppermute x5, waiting for transfers between devices, over_rows(): return lax.ppermute(a, ('row', 'col'), rows(f))  7.47 us
    pallas_call x9, Pallas kernels, call(): pl.pallas_call(kernel, out_shape=outs, in_specs=[pl.BlockSpec(memory_spac...  6.17 us
    all_to_all x1, starting transfers between devices, over_chips(): lax.all_to_all(a, 'col', 0, 0, tiled=True, axis_index_groups=OVER_CHIPS)  5.18 us
    unnamed x6, local copies, waits for them, and re-layouts  2.06 us
  transfers between devices with their start and end apart: 21, of which 9 were waited for; matrix products, arithmetic and copies ran while one was open for 0% of the time, Pallas kernels for 7%

profile of v2, /device:TPU:2, one launch (start us, length us, event | category | flops | bytes accessed | tf_op | source)
XLA Modules:
  0.0 70.6 jit_solution(13335492415375219395)
XLA Ops:
  0.0 0.7 copy-done.2
  0.7 3.2 %collective-permute-start = (f32[8,128]{1,0:T(8,128)S(1)}, f32[8,128]{1,0:T(8,128)S(1)}, u32[]{:S(2)}, u32[]{:S(2)}) collective-permute-start(f32[8,128]{1,0:T(8,128)S(1)} %shard_map.38.a), channel_id=1, source_target_pairs={{0,16},{1,17},{2,18},{3,19},{4,20},{5,21},{6,22},{7,23},{8,24},{9,... | collective-permute-start | bytes 12296 | tf_op jit(solution)/shard_map/ppermute | solution.py:50
  3.9 1.4 %copy-done = f32[32,11520]{1,0:T(8,128)S(1)} copy-done((f32[32,11520]{1,0:T(8,128)S(1)}, f32[32,11520]{1,0:T(8,128)}, u32[]{:S(2)}) %copy-start) | copy-done | bytes 1474584
  5.3 1.2 %shard_map.37 = f32[8,360,128]{2,1,0:T(8,128)} custom-call(f32[32,11520]{1,0:T(8,128)S(1)} %copy-done), custom_call_target="tpu_custom_call" | custom-call | bytes 2949120 | tf_op jit(solution)/shard_map/pallas_call | solution.py:185
  6.5 5.2 %all-to-all-start = ((f32[8,360,128]{2,1,0:T(8,128)}), f32[8,360,128]{2,1,0:T(8,128)S(1)}, u32[]{:S(2)}, u32[]{:S(2)}) async-start(f32[8,360,128]{2,1,0:T(8,128)} %shard_map.37), calls=%async_computation | async-start | bytes 2949120 | tf_op jit(solution)/shard_map/all_to_all | solution.py:38
  11.7 7.2 %collective-permute-start.1 = (f32[16,128]{1,0:T(8,128)S(1)}, f32[16,128]{1,0:T(8,128)S(1)}, u32[]{:S(2)}, u32[]{:S(2)}) collective-permute-start(f32[16,128]{1,0:T(8,128)S(1)} %shard_map.39.a), channel_id=1, source_target_pairs={{0,128},{1,129},{2,130},{3,131},{4,132},{5,133},{6,134},{7,135},{8... | collective-permute-start | bytes 24584 | tf_op jit(solution)/shard_map/ppermute | solution.py:50
  18.8 1.6 %collective-permute-done.1.b = f32[16,128]{1,0:T(8,128)S(1)} collective-permute-done((f32[16,128]{1,0:T(8,128)S(1)}, f32[16,128]{1,0:T(8,128)S(1)}, u32[]{:S(2)}, u32[]{:S(2)}) %collective-permute-start.1) | collective-permute-done | bytes 8224 | tf_op jit(solution)/shard_map/ppermute | solution.py:50
  20.5 1.0 %collective-permute-start.2 = (f32[32,128]{1,0:T(8,128)S(1)}, f32[32,128]{1,0:T(8,128)S(1)}, u32[]{:S(2)}, u32[]{:S(2)}) collective-permute-start(f32[32,128]{1,0:T(8,128)S(1)} %shard_map.40.refs_0_), channel_id=1, source_target_pairs={{0,32},{1,33},{2,34},{3,35},{4,36},{5,37},{6,38},{7,39},{8,40},{9,... | collective-permute-start | bytes 49160 | tf_op jit(solution)/shard_map/ppermute | solution.py:50
  21.5 3.6 %collective-permute-start.3 = (f32[32,128]{1,0:T(8,128)S(1)}, f32[32,128]{1,0:T(8,128)S(1)}, u32[]{:S(2)}, u32[]{:S(2)}) collective-permute-start(f32[32,128]{1,0:T(8,128)S(1)} %shard_map.40.refs_0_), channel_id=1, source_target_pairs={{0,224},{1,225},{2,226},{3,227},{4,228},{5,229},{6,230},{7,231},{8... | collective-permute-start | bytes 49160 | tf_op jit(solution)/shard_map/ppermute | solution.py:50
  25.1 1.7 %collective-permute-done.2.refs_1_ = f32[32,128]{1,0:T(8,128)S(1)} collective-permute-done((f32[32,128]{1,0:T(8,128)S(1)}, f32[32,128]{1,0:T(8,128)S(1)}, u32[]{:S(2)}, u32[]{:S(2)}) %collective-permute-start.2) | collective-permute-done | bytes 16416 | tf_op jit(solution)/shard_map/ppermute | solution.py:50
  26.8 4.1 %collective-permute-done.4.refs_3_ = f32[32,128]{1,0:T(8,128)S(1)} collective-permute-done((f32[32,128]{1,0:T(8,128)S(1)}, f32[32,128]{1,0:T(8,128)S(1)}, u32[]{:S(2)}, u32[]{:S(2)}) %collective-permute-start.4) | collective-permute-done | bytes 16416 | tf_op jit(solution)/shard_map/ppermute | solution.py:50
  31.1 1.6 %collective-permute-start.6 = (f32[128,128]{1,0:T(8,128)S(1)}, f32[128,128]{1,0:T(8,128)S(1)}, u32[]{:S(2)}, u32[]{:S(2)}) collective-permute-start(f32[128,128]{1,0:T(8,128)S(1)} %shard_map.41.refs_0_), channel_id=1, source_target_pairs={{0,2},{1,3},{2,0},{3,1},{4,6},{5,7},{6,4},{7,5},{8,10},{9,11},{10,... | collective-permute-start | bytes 196616 | tf_op jit(solution)/shard_map/ppermute | solution.py:42
  32.6 0.6 collective-permute-start.10
  33.2 2.7 %collective-permute-start.11 = (f32[128,128]{1,0:T(8,128)S(1)}, f32[128,128]{1,0:T(8,128)S(1)}, u32[]{:S(2)}, u32[]{:S(2)}) collective-permute-start(f32[128,128]{1,0:T(8,128)S(1)} %shard_map.41.refs_0_), channel_id=1, source_target_pairs={{0,14},{1,15},{2,12},{3,13},{4,2},{5,3},{6,0},{7,1},{8,6},{9,7},{1... | collective-permute-start | bytes 196616 | tf_op jit(solution)/shard_map/ppermute | solution.py:42
  35.8 0.6 collective-permute-start.8
  36.4 1.5 %collective-permute-start.9 = (f32[128,128]{1,0:T(8,128)S(1)}, f32[128,128]{1,0:T(8,128)S(1)}, u32[]{:S(2)}, u32[]{:S(2)}) collective-permute-start(f32[128,128]{1,0:T(8,128)S(1)} %shard_map.41.refs_0_), channel_id=1, source_target_pairs={{0,6},{1,7},{2,4},{3,5},{4,10},{5,11},{6,8},{7,9},{8,14},{9,15},{1... | collective-permute-start | bytes 196616 | tf_op jit(solution)/shard_map/ppermute | solution.py:42
  37.9 1.7 %shard_map.42 = (f32[360,128]{1,0:T(8,128)S(1)}, f32[360,128]{1,0:T(8,128)S(1)}, bf16[512,1536]{1,0:T(8,128)(2,1)S(1)}, bf16[512,1536]{1,0:T(8,128)(2,1)S(1)}) custom-call(f32[8,360,128]{2,1,0:T(8,128)S(1)} %all-to-all-done.mine, f32[8,360,128]{2,1,0:T(8,128)S(1)} %collective-permute-done.5.other, f32[128,128]{1,0:T(8,128)S(1)} %shard_map.41.refs_0_, ...), custom_call_target="tpu_custom_call" | custom-call | flops 283115520 | bytes 6594560 | tf_op jit(solution)/shard_map/pallas_call | solution.py:185
  39.6 0.6 collective-permute-start.7
  40.3 1.4 %collective-permute-done.9.refs_1_ = f32[128,128]{1,0:T(8,128)S(1)} collective-permute-done((f32[128,128]{1,0:T(8,128)S(1)}, f32[128,128]{1,0:T(8,128)S(1)}, u32[]{:S(2)}, u32[]{:S(2)}) %collective-permute-start.9) | collective-permute-done | bytes 65568 | tf_op jit(solution)/shard_map/ppermute | solution.py:42
  41.8 0.8 %shard_map.43 = (f32[360,128]{1,0:T(8,128)S(1)}, f32[360,128]{1,0:T(8,128)S(1)}, f32[360,128]{1,0:T(8,128)S(1)}, f32[360,128]{1,0:T(8,128)S(1)}) custom-call(bf16[512,1536]{1,0:T(8,128)(2,1)S(1)} %get-tuple-element.31.v_hi, bf16[512,1536]{1,0:T(8,128)(2,1)S(1)} %get-tuple-element.32.v_lo, f32[128,128]{1,0:T(8,128)S(1)} %collective-permute-done.8.refs_0_, ...), custom_call_target="tpu_custom_call" | custom-call | flops 566231040 | bytes 4145152 | tf_op jit(solution)/shard_map/pallas_call | solution.py:185
  42.6 0.9 %collective-permute-start.12 = (f32[360,128]{1,0:T(8,128)S(1)}, f32[360,128]{1,0:T(8,128)S(1)}, u32[]{:S(2)}, u32[]{:S(2)}) collective-permute-start(f32[360,128]{1,0:T(8,128)S(1)} %get-tuple-element.29), channel_id=1, source_target_pairs={{0,4},{1,5},{2,6},{3,7},{4,8},{5,9},{6,10},{7,11},{8,12},{9,13},{1... | collective-permute-start | bytes 552968 | tf_op jit(solution)/shard_map/ppermute | solution.py:42
  43.5 3.9 %collective-permute-start.14 = (f32[128,128]{1,0:T(8,128)S(1)}, f32[128,128]{1,0:T(8,128)S(1)}, u32[]{:S(2)}, u32[]{:S(2)}) collective-permute-start(f32[128,128]{1,0:T(8,128)S(1)} %shard_map.41.refs_0_), channel_id=1, source_target_pairs={{0,8},{1,9},{2,10},{3,11},{4,12},{5,13},{6,14},{7,15},{8,0},{9,1},... | collective-permute-start | bytes 196616 | tf_op jit(solution)/shard_map/ppermute | solution.py:42
  47.4 0.9 %collective-permute-start.15 = (f32[128,128]{1,0:T(8,128)S(1)}, f32[128,128]{1,0:T(8,128)S(1)}, u32[]{:S(2)}, u32[]{:S(2)}) collective-permute-start(f32[128,128]{1,0:T(8,128)S(1)} %shard_map.41.refs_0_), channel_id=1, source_target_pairs={{0,10},{1,11},{2,8},{3,9},{4,14},{5,15},{6,12},{7,13},{8,2},{9,3},... | collective-permute-start | bytes 196616 | tf_op jit(solution)/shard_map/ppermute | solution.py:42
  48.3 1.6 %collective-permute-start.13 = (f32[360,128]{1,0:T(8,128)S(1)}, f32[360,128]{1,0:T(8,128)S(1)}, u32[]{:S(2)}, u32[]{:S(2)}) collective-permute-start(f32[360,128]{1,0:T(8,128)S(1)} %get-tuple-element.30), channel_id=1, source_target_pairs={{0,6},{1,7},{2,4},{3,5},{4,10},{5,11},{6,8},{7,9},{8,14},{9,15},{1... | collective-permute-start | bytes 552968 | tf_op jit(solution)/shard_map/ppermute | solution.py:42
  50.3 3.7 %collective-permute-start.19 = (f32[360,128]{1,0:T(8,128)S(1)}, f32[360,128]{1,0:T(8,128)S(1)}, u32[]{:S(2)}, u32[]{:S(2)}) collective-permute-start(f32[360,128]{1,0:T(8,128)S(1)} %get-tuple-element.36), channel_id=1, source_target_pairs={{0,14},{1,15},{2,12},{3,13},{4,2},{5,3},{6,0},{7,1},{8,6},{9,7},{1... | collective-permute-start | bytes 552968 | tf_op jit(solution)/shard_map/ppermute | solution.py:42
  54.0 1.5 %collective-permute-done.15.refs_1_ = f32[128,128]{1,0:T(8,128)S(1)} collective-permute-done((f32[128,128]{1,0:T(8,128)S(1)}, f32[128,128]{1,0:T(8,128)S(1)}, u32[]{:S(2)}, u32[]{:S(2)}) %collective-permute-start.15) | collective-permute-done | bytes 65568 | tf_op jit(solution)/shard_map/ppermute | solution.py:42
  55.5 1.0 %shard_map.44 = (f32[360,128]{1,0:T(8,128)S(1)}, f32[360,128]{1,0:T(8,128)S(1)}) custom-call(bf16[512,1536]{1,0:T(8,128)(2,1)S(1)} %get-tuple-element.31.v_hi, bf16[512,1536]{1,0:T(8,128)(2,1)S(1)} %get-tuple-element.32.v_lo, f32[128,128]{1,0:T(8,128)S(1)} %collective-permute-done.14.refs_0_, f32[128,128]{1,0:T(8,128)S(1)} %collective-permute-done.15.refs_1_), custom_call_target="tpu_custom_call" | custom-call | flops 283115520 | bytes 3645440 | tf_op jit(solution)/shard_map/pallas_call | solution.py:185
  56.4 0.8 %collective-permute-start.16 = (f32[360,128]{1,0:T(8,128)S(1)}, f32[360,128]{1,0:T(8,128)S(1)}, u32[]{:S(2)}, u32[]{:S(2)}) collective-permute-start(f32[360,128]{1,0:T(8,128)S(1)} %get-tuple-element.33), channel_id=1, source_target_pairs={{0,8},{1,9},{2,10},{3,11},{4,12},{5,13},{6,14},{7,15},{8,0},{9,1},... | collective-permute-start | bytes 552968 | tf_op jit(solution)/shard_map/ppermute | solution.py:42
  57.2 4.3 %collective-permute-start.17 = (f32[360,128]{1,0:T(8,128)S(1)}, f32[360,128]{1,0:T(8,128)S(1)}, u32[]{:S(2)}, u32[]{:S(2)}) collective-permute-start(f32[360,128]{1,0:T(8,128)S(1)} %get-tuple-element.34), channel_id=1, source_target_pairs={{0,10},{1,11},{2,8},{3,9},{4,14},{5,15},{6,12},{7,13},{8,2},{9,3},... | collective-permute-start | bytes 552968 | tf_op jit(solution)/shard_map/ppermute | solution.py:42
  61.8 4.4 %collective-permute-done.16.refs_4_ = f32[360,128]{1,0:T(8,128)S(1)} collective-permute-done((f32[360,128]{1,0:T(8,128)S(1)}, f32[360,128]{1,0:T(8,128)S(1)}, u32[]{:S(2)}, u32[]{:S(2)}) %collective-permute-start.16) | collective-permute-done | bytes 184352 | tf_op jit(solution)/shard_map/ppermute | solution.py:42
  66.3 2.9 %collective-permute-done.17.refs_5_ = f32[360,128]{1,0:T(8,128)S(1)} collective-permute-done((f32[360,128]{1,0:T(8,128)S(1)}, f32[360,128]{1,0:T(8,128)S(1)}, u32[]{:S(2)}, u32[]{:S(2)}) %collective-permute-start.17) | collective-permute-done | bytes 184352 | tf_op jit(solution)/shard_map/ppermute | solution.py:42
  69.1 1.4 %shard_map.45 = f32[32,11520]{1,0:T(8,128)} custom-call(f32[360,128]{1,0:T(8,128)S(1)} %get-tuple-element.24.refs_0_, f32[360,128]{1,0:T(8,128)S(1)} %collective-permute-done.7.refs_1_, f32[360,128]{1,0:T(8,128)S(1)} %collective-permute-done.12.refs_2_, f32[360,128]{1,0:T(8,128)S(1)} %collective-permute-done.13.refs_3_, ...), custom_call_target="tpu_custom_call" | custom-call | bytes 4423680 | tf_op jit(solution)/shard_map/pallas_call | solution.py:185
  (25 shorter events, 1.0 us)
Async XLA Ops:
  0.0 0.7 copy-start.2
  0.7 5.8 %collective-permute-start = (f32[8,128]{1,0:T(8,128)S(1)}, f32[8,128]{1,0:T(8,128)S(1)}, u32[]{:S(2)}, u32[]{:S(2)}) collective-permute-start(f32[8,128]{1,0:T(8,128)S(1)} %shard_map.38.a), channel_id=1, source_target_pairs={{0,16},{1,17},{2,18},{3,19},{4,20},{5,21},{6,22},{7,23},{8,24},{9,... | collective-permute-start | bytes 12296 | tf_op jit(solution)/shard_map/ppermute | solution.py:50
  3.9 1.4 %copy-start = (f32[32,11520]{1,0:T(8,128)S(1)}, f32[32,11520]{1,0:T(8,128)}, u32[]{:S(2)}) copy-start(f32[32,11520]{1,0:T(8,128)} %v.1) | copy-start | bytes 4423684
  6.5 24.5 %all-to-all-start = ((f32[8,360,128]{2,1,0:T(8,128)}), f32[8,360,128]{2,1,0:T(8,128)S(1)}, u32[]{:S(2)}, u32[]{:S(2)}) async-start(f32[8,360,128]{2,1,0:T(8,128)} %shard_map.37), calls=%async_computation | async-start | bytes 2949120 | tf_op jit(solution)/shard_map/all_to_all | solution.py:38
  11.7 8.8 %collective-permute-start.1 = (f32[16,128]{1,0:T(8,128)S(1)}, f32[16,128]{1,0:T(8,128)S(1)}, u32[]{:S(2)}, u32[]{:S(2)}) collective-permute-start(f32[16,128]{1,0:T(8,128)S(1)} %shard_map.39.a), channel_id=1, source_target_pairs={{0,128},{1,129},{2,130},{3,131},{4,132},{5,133},{6,134},{7,135},{8... | collective-permute-start | bytes 24584 | tf_op jit(solution)/shard_map/ppermute | solution.py:50
  20.5 6.3 %collective-permute-start.2 = (f32[32,128]{1,0:T(8,128)S(1)}, f32[32,128]{1,0:T(8,128)S(1)}, u32[]{:S(2)}, u32[]{:S(2)}) collective-permute-start(f32[32,128]{1,0:T(8,128)S(1)} %shard_map.40.refs_0_), channel_id=1, source_target_pairs={{0,32},{1,33},{2,34},{3,35},{4,36},{5,37},{6,38},{7,39},{8,40},{9,... | collective-permute-start | bytes 49160 | tf_op jit(solution)/shard_map/ppermute | solution.py:50
  21.5 5.3 %collective-permute-start.3 = (f32[32,128]{1,0:T(8,128)S(1)}, f32[32,128]{1,0:T(8,128)S(1)}, u32[]{:S(2)}, u32[]{:S(2)}) collective-permute-start(f32[32,128]{1,0:T(8,128)S(1)} %shard_map.40.refs_0_), channel_id=1, source_target_pairs={{0,224},{1,225},{2,226},{3,227},{4,228},{5,229},{6,230},{7,231},{8... | collective-permute-start | bytes 49160 | tf_op jit(solution)/shard_map/ppermute | solution.py:50
  25.1 5.8 %collective-permute-start.4 = (f32[32,128]{1,0:T(8,128)S(1)}, f32[32,128]{1,0:T(8,128)S(1)}, u32[]{:S(2)}, u32[]{:S(2)}) collective-permute-start(f32[32,128]{1,0:T(8,128)S(1)} %shard_map.40.refs_0_), channel_id=1, source_target_pairs={{0,64},{1,193},{2,66},{3,195},{4,68},{5,197},{6,70},{7,199},{8,72}... | collective-permute-start | bytes 49160 | tf_op jit(solution)/shard_map/ppermute | solution.py:50
  31.0 7.0 %collective-permute-start.5 = (f32[8,360,128]{2,1,0:T(8,128)S(1)}, f32[8,360,128]{2,1,0:T(8,128)S(1)}, u32[]{:S(2)}, u32[]{:S(2)}) collective-permute-start(f32[8,360,128]{2,1,0:T(8,128)S(1)} %all-to-all-done.mine), channel_id=1, source_target_pairs={{0,1},{1,0},{2,3},{3,2},{4,5},{5,4},{6,7},{7,6},{8,9},{9,8},{10,11... | collective-permute-start | bytes 4423688 | tf_op jit(solution)/shard_map/ppermute | solution.py:46
  31.1 5.4 %collective-permute-start.6 = (f32[128,128]{1,0:T(8,128)S(1)}, f32[128,128]{1,0:T(8,128)S(1)}, u32[]{:S(2)}, u32[]{:S(2)}) collective-permute-start(f32[128,128]{1,0:T(8,128)S(1)} %shard_map.41.refs_0_), channel_id=1, source_target_pairs={{0,2},{1,3},{2,0},{3,1},{4,6},{5,7},{6,4},{7,5},{8,10},{9,11},{10,... | collective-permute-start | bytes 196616 | tf_op jit(solution)/shard_map/ppermute | solution.py:42
  32.6 7.6 %collective-permute-start.10 = (f32[128,128]{1,0:T(8,128)S(1)}, f32[128,128]{1,0:T(8,128)S(1)}, u32[]{:S(2)}, u32[]{:S(2)}) collective-permute-start(f32[128,128]{1,0:T(8,128)S(1)} %shard_map.41.refs_0_), channel_id=1, source_target_pairs={{0,12},{1,13},{2,14},{3,15},{4,0},{5,1},{6,2},{7,3},{8,4},{9,5},{1... | collective-permute-start | bytes 196616 | tf_op jit(solution)/shard_map/ppermute | solution.py:42
  33.2 7.0 %collective-permute-start.11 = (f32[128,128]{1,0:T(8,128)S(1)}, f32[128,128]{1,0:T(8,128)S(1)}, u32[]{:S(2)}, u32[]{:S(2)}) collective-permute-start(f32[128,128]{1,0:T(8,128)S(1)} %shard_map.41.refs_0_), channel_id=1, source_target_pairs={{0,14},{1,15},{2,12},{3,13},{4,2},{5,3},{6,0},{7,1},{8,6},{9,7},{1... | collective-permute-start | bytes 196616 | tf_op jit(solution)/shard_map/ppermute | solution.py:42
  35.8 4.5 %collective-permute-start.8 = (f32[128,128]{1,0:T(8,128)S(1)}, f32[128,128]{1,0:T(8,128)S(1)}, u32[]{:S(2)}, u32[]{:S(2)}) collective-permute-start(f32[128,128]{1,0:T(8,128)S(1)} %shard_map.41.refs_0_), channel_id=1, source_target_pairs={{0,4},{1,5},{2,6},{3,7},{4,8},{5,9},{6,10},{7,11},{8,12},{9,13},{1... | collective-permute-start | bytes 196616 | tf_op jit(solution)/shard_map/ppermute | solution.py:42
  36.4 5.3 %collective-permute-start.9 = (f32[128,128]{1,0:T(8,128)S(1)}, f32[128,128]{1,0:T(8,128)S(1)}, u32[]{:S(2)}, u32[]{:S(2)}) collective-permute-start(f32[128,128]{1,0:T(8,128)S(1)} %shard_map.41.refs_0_), channel_id=1, source_target_pairs={{0,6},{1,7},{2,4},{3,5},{4,10},{5,11},{6,8},{7,9},{8,14},{9,15},{1... | collective-permute-start | bytes 196616 | tf_op jit(solution)/shard_map/ppermute | solution.py:42
  39.6 10.3 %collective-permute-start.7 = (f32[360,128]{1,0:T(8,128)S(1)}, f32[360,128]{1,0:T(8,128)S(1)}, u32[]{:S(2)}, u32[]{:S(2)}) collective-permute-start(f32[360,128]{1,0:T(8,128)S(1)} %get-tuple-element.27), channel_id=1, source_target_pairs={{0,2},{1,3},{2,0},{3,1},{4,6},{5,7},{6,4},{7,5},{8,10},{9,11},{10,... | collective-permute-start | bytes 552968 | tf_op jit(solution)/shard_map/ppermute | solution.py:42
  42.6 14.6 %collective-permute-start.12 = (f32[360,128]{1,0:T(8,128)S(1)}, f32[360,128]{1,0:T(8,128)S(1)}, u32[]{:S(2)}, u32[]{:S(2)}) collective-permute-start(f32[360,128]{1,0:T(8,128)S(1)} %get-tuple-element.29), channel_id=1, source_target_pairs={{0,4},{1,5},{2,6},{3,7},{4,8},{5,9},{6,10},{7,11},{8,12},{9,13},{1... | collective-permute-start | bytes 552968 | tf_op jit(solution)/shard_map/ppermute | solution.py:42
  43.5 6.8 %collective-permute-start.14 = (f32[128,128]{1,0:T(8,128)S(1)}, f32[128,128]{1,0:T(8,128)S(1)}, u32[]{:S(2)}, u32[]{:S(2)}) collective-permute-start(f32[128,128]{1,0:T(8,128)S(1)} %shard_map.41.refs_0_), channel_id=1, source_target_pairs={{0,8},{1,9},{2,10},{3,11},{4,12},{5,13},{6,14},{7,15},{8,0},{9,1},... | collective-permute-start | bytes 196616 | tf_op jit(solution)/shard_map/ppermute | solution.py:42
  47.4 8.1 %collective-permute-start.15 = (f32[128,128]{1,0:T(8,128)S(1)}, f32[128,128]{1,0:T(8,128)S(1)}, u32[]{:S(2)}, u32[]{:S(2)}) collective-permute-start(f32[128,128]{1,0:T(8,128)S(1)} %shard_map.41.refs_0_), channel_id=1, source_target_pairs={{0,10},{1,11},{2,8},{3,9},{4,14},{5,15},{6,12},{7,13},{8,2},{9,3},... | collective-permute-start | bytes 196616 | tf_op jit(solution)/shard_map/ppermute | solution.py:42
  48.3 13.3 %collective-permute-start.13 = (f32[360,128]{1,0:T(8,128)S(1)}, f32[360,128]{1,0:T(8,128)S(1)}, u32[]{:S(2)}, u32[]{:S(2)}) collective-permute-start(f32[360,128]{1,0:T(8,128)S(1)} %get-tuple-element.30), channel_id=1, source_target_pairs={{0,6},{1,7},{2,4},{3,5},{4,10},{5,11},{6,8},{7,9},{8,14},{9,15},{1... | collective-permute-start | bytes 552968 | tf_op jit(solution)/shard_map/ppermute | solution.py:42
  49.9 11.7 %collective-permute-start.18 = (f32[360,128]{1,0:T(8,128)S(1)}, f32[360,128]{1,0:T(8,128)S(1)}, u32[]{:S(2)}, u32[]{:S(2)}) collective-permute-start(f32[360,128]{1,0:T(8,128)S(1)} %get-tuple-element.35), channel_id=1, source_target_pairs={{0,12},{1,13},{2,14},{3,15},{4,0},{5,1},{6,2},{7,3},{8,4},{9,5},{1... | collective-permute-start | bytes 552968 | tf_op jit(solution)/shard_map/ppermute | solution.py:42
  50.3 18.8 %copy-start.1 = (f32[32,11520]{1,0:T(8,128)S(1)}, f32[32,11520]{1,0:T(8,128)}, u32[]{:S(2)}) copy-start(f32[32,11520]{1,0:T(8,128)} %refs_8_.1) | copy-start | bytes 4423684
  50.3 11.5 %collective-permute-start.19 = (f32[360,128]{1,0:T(8,128)S(1)}, f32[360,128]{1,0:T(8,128)S(1)}, u32[]{:S(2)}, u32[]{:S(2)}) collective-permute-start(f32[360,128]{1,0:T(8,128)S(1)} %get-tuple-element.36), channel_id=1, source_target_pairs={{0,14},{1,15},{2,12},{3,13},{4,2},{5,3},{6,0},{7,1},{8,6},{9,7},{1... | collective-permute-start | bytes 552968 | tf_op jit(solution)/shard_map/ppermute | solution.py:42
  56.4 9.8 %collective-permute-start.16 = (f32[360,128]{1,0:T(8,128)S(1)}, f32[360,128]{1,0:T(8,128)S(1)}, u32[]{:S(2)}, u32[]{:S(2)}) collective-permute-start(f32[360,128]{1,0:T(8,128)S(1)} %get-tuple-element.33), channel_id=1, source_target_pairs={{0,8},{1,9},{2,10},{3,11},{4,12},{5,13},{6,14},{7,15},{8,0},{9,1},... | collective-permute-start | bytes 552968 | tf_op jit(solution)/shard_map/ppermute | solution.py:42
  57.2 11.9 %collective-permute-start.17 = (f32[360,128]{1,0:T(8,128)S(1)}, f32[360,128]{1,0:T(8,128)S(1)}, u32[]{:S(2)}, u32[]{:S(2)}) collective-permute-start(f32[360,128]{1,0:T(8,128)S(1)} %get-tuple-element.34), channel_id=1, source_target_pairs={{0,10},{1,11},{2,8},{3,9},{4,14},{5,15},{6,12},{7,13},{8,2},{9,3},... | collective-permute-start | bytes 552968 | tf_op jit(solution)/shard_map/ppermute | solution.py:42

commit v3 on v2

--- a/solution.py
+++ b/solution.py
@@ -77,8 +77,10 @@
         msgs[q, TILES * ROWS :, :] = folded
 
 
-def tile_kernel(a, out):
-    out[...] = jnp.concatenate([a[i : i + 1, c * LANES : (c + 1) * LANES] for i in range(2) for c in range(4)], axis=0)
+def tiles_kernel(a, b, out):
+    for n, part in enumerate((a, b)):
+        rows = [part[i : i + 1, c * LANES : (c + 1) * LANES] for i in range(2) for c in range(4)]
+        out[8 * n : 8 * n + 8, :] = jnp.concatenate(rows, axis=0)
 
 
 def join_kernel(a, b, out):
@@ -134,23 +136,26 @@
 def amplitude_rows(amps):
     his, los = [], []
     for amp in amps:
-        parts = [split(amp[pl.ds(c, ROWS, stride=4), :]) for c in range(4)]
-        his.append(jnp.concatenate([p[0] for p in parts], axis=1))
-        los.append(jnp.concatenate([p[1] for p in parts], axis=1))
+        for h in range(2):
+            parts = [split(amp[pl.ds(128 * h + c, ROWS, stride=4), :]) for c in range(4)]
+            his.append(jnp.concatenate([p[0] for p in parts], axis=1))
+            los.append(jnp.concatenate([p[1] for p in parts], axis=1))
     return jnp.concatenate(his, axis=0), jnp.concatenate(los, axis=0)
 
 
-def first_kernel(n, mine, other, *refs):
-    amps, msgs, (v_hi, v_lo) = refs[:n], refs[n : 2 * n], refs[2 * n :]
+def first_kernel(mine, other, amp, *refs):
+    msgs, (v_hi, v_lo) = refs[:2], refs[2:4]
     _, _, k, _ = here()
     for q in range(8):
         unpack(mine.at[q], v_hi, v_lo, (2 * q + k) * ROWS)
         unpack(other.at[q], v_hi, v_lo, (2 * q + 1 - k) * ROWS)
-    ladder(*amplitude_rows(amps), v_hi, v_lo, msgs)
+    t_hi, t_lo = amplitude_rows([amp])
+    ladder(t_hi, t_lo, v_hi, v_lo, msgs)
 
 
 def later_kernel(n, v_hi, v_lo, *refs):
-    ladder(*amplitude_rows(refs[:n]), v_hi, v_lo, refs[n:])
+    t_hi, t_lo = amplitude_rows(refs[:n])
+    ladder(t_hi, t_lo, v_hi, v_lo, refs[n:])
 
 
 def chip(o, sign, relative):
@@ -197,15 +202,15 @@
     return jax.ShapeDtypeStruct(shape, jnp.float32)
 
 
-GROUPS = [[(0, 0), (0, 1)], [(1, 0), (1, 1), (3, 0), (3, 1)], [(2, 0), (2, 1)]]
+GROUPS = ((2,), (1, 3))
 
 
 def body(amplitudes, integrals, previous):
     msg, stack = f32(MSG, LANES), f32(8, MSG, LANES)
-    tile = call(tile_kernel, [f32(8, LANES)], [amplitudes])[0]
-    part = call(join_kernel, [f32(16, LANES)], [tile, over_rows(tile, lambda z, y, k: (z, y + 1))])[0]
+    beside = over_rows(amplitudes, lambda z, y, k: (z, y + 1))
     sent = call(pack_kernel, [stack], [integrals])[0]
-    sent, part = lax.optimization_barrier((sent, part))
+    sent, beside = lax.optimization_barrier((sent, beside))
+    part = call(tiles_kernel, [f32(16, LANES)], [amplitudes, beside])[0]
     part = call(join_kernel, [f32(32, LANES)], [part, over_rows(part, lambda z, y, k: (z + 4, y))])[0]
     parts = [
         part,
@@ -214,27 +219,23 @@
         over_rows(part, lambda z, y, k: (z + 2 - 4 * k, y)),
     ]
     own = call(collect_kernel, [f32(128, LANES)], parts)[0]
-    mine, _ = lax.optimization_barrier((over_chips(sent), own))
-    amps = {o: to_chip(own, *o) for o in [(0, 1), (1, 0), (3, 0), (1, 1), (3, 1), (2, 0), (2, 1)]}
-    amps[(0, 0)] = own
+    pair = call(join_kernel, [f32(256, LANES)], [own, to_chip(own, 0, 1)])[0]
+    mine, _ = lax.optimization_barrier((over_chips(sent), pair))
     other = swap_cores(mine)
-    flops = 3 * 2 * 32 * 512 * 1440
+    amps = {dx: to_chip(pair, dx, 0) for group in GROUPS for dx in group}
+    flops = 3 * 2 * 64 * 512 * 1440
     v_shape = jax.ShapeDtypeStruct((512, 12 * LANES), jnp.bfloat16)
-    back = {}
-    for i, group in enumerate(GROUPS):
+    near, far, *v = call(first_kernel, [msg] * 2 + [v_shape] * 2, [mine, other, pair], flops, limit=32)
+    back = {(0, 0): near, (0, 1): to_chip(far, 0, 1)}
+    for group in GROUPS:
         n = len(group)
-        rows = [amps[o] for o in group]
-        if i == 0:
-            kernel, outs, args = first_kernel, [msg] * n + [v_shape] * 2, [mine, other] + rows
-        else:
-            if i == 2:
-                *v, back[(0, 1)] = lax.optimization_barrier((*v, back[(0, 1)]))
-            kernel, outs, args = later_kernel, [msg] * n, v + rows
-        out = call(functools.partial(kernel, n), outs, args, n * flops, limit=32)
-        v = list(out[n:]) if i == 0 else v
-        for (dx, dy), m in zip(group, out):
-            o = ((4 - dx) % 4, dy)
-            back[o] = m if o == (0, 0) else to_chip(m, *o)
+        if group == GROUPS[-1]:
+            *v, back[(0, 1)] = lax.optimization_barrier((*v, back[(0, 1)]))
+        args = list(v) + [amps[dx] for dx in group]
+        out = call(functools.partial(later_kernel, n), [msg] * 2 * n, args, n * flops, limit=32)
+        for j, dx in enumerate(group):
+            for dy in range(2):
+                back[(4 - dx, dy)] = to_chip(out[2 * j + dy], 4 - dx, dy)
     return call(add_rel_kernel, [f32(*previous.shape)], [back[o] for o in OFFSETS] + [previous])[0]
 
 

time: 70.8 us -> 68.5 us (0.968)
  starting transfers between devices: 44.2 us -> 41.7 us
  waiting for transfers between devices: 18.1 us -> 19.1 us
    ppermute x14 -> x11, starting transfers between devices: 23.9 us -> 21.1 us  [to_chip(): return lax.ppermute(a, 'col', cols(lambda x, y, k: (x + dx, y + dy, k)))]
    ppermute x1, waiting for transfers between devices: 0.01 us -> 1.1 us  [swap_cores(): return lax.ppermute(a, 'col', cols(lambda x, y, k: (x, y, k + 1)))]
    ppermute x14 -> x11, waiting for transfers between devices: 10.6 us -> 10.5 us  [to_chip(): return lax.ppermute(a, 'col', cols(lambda x, y, k: (x + dx, y + dy, k)))]
  transfers between devices with their start and end apart: 21 -> 18, of which waited for: 9 -> 8; matrix products, arithmetic and copies ran while one was open for 0% -> 0% of each run, Pallas kernels for 7% -> 7%
where the time goes in v3:
time: 68.5 us; the launch traced here: 68.4 us
  starting transfers between devices  41.7 us (61%)
  waiting for transfers between devices  19.1 us (28%)
  Pallas kernels  6.19 us (9%)
  local copies, waits for them, and re-layouts  1.38 us (2%)
    ppermute x11, starting transfers between devices, to_chip(): return lax.ppermute(a, 'col', cols(lambda x, y, k: (x + dx, y + dy, k)))  21.1 us
    ppermute x5, starting transfers between devices, over_rows(): return lax.ppermute(a, ('row', 'col'), rows(f))  15.1 us
    ppermute x11, waiting for transfers between devices, to_chip(): return lax.ppermute(a, 'col', cols(lambda x, y, k: (x + dx, y + dy, k)))  10.5 us
    ppermute x5, waiting for transfers between devices, over_rows(): return lax.ppermute(a, ('row', 'col'), rows(f))  7.48 us
    pallas_call x9, Pallas kernels, call(): pl.pallas_call(kernel, out_shape=outs, in_specs=[pl.BlockSpec(memory_spac...  6.19 us
    all_to_all x1, starting transfers between devices, over_chips(): lax.all_to_all(a, 'col', 0, 0, tiled=True, axis_index_groups=OVER_CHIPS)  5.38 us
    unnamed x6, local copies, waits for them, and re-layouts  1.38 us
  transfers between devices with their start and end apart: 18, of which 8 were waited for; matrix products, arithmetic and copies ran while one was open for 0% of the time, Pallas kernels for 7%

profile of v3, /device:TPU:2, one launch (start us, length us, event | category | flops | bytes accessed | tf_op | source)
XLA Modules:
  0.0 68.4 jit_solution(9333355025363555937)
XLA Ops:
  0.0 3.2 %collective-permute-start = (f32[2,512]{1,0:T(2,128)}, f32[2,512]{1,0:T(2,128)S(1)}, u32[]{:S(2)}, u32[]{:S(2)}) collective-permute-start(f32[2,512]{1,0:T(2,128)} %a.1), channel_id=1, source_target_pairs={{0,16},{1,17},{2,18},{3,19},{4,20},{5,21},{6,22},{7,23},{8,24},{9,... | collective-permute-start | bytes 12296 | tf_op jit(solution)/shard_map/ppermute | solution.py:50
  3.2 1.4 %copy-done = f32[32,11520]{1,0:T(8,128)S(1)} copy-done((f32[32,11520]{1,0:T(8,128)S(1)}, f32[32,11520]{1,0:T(8,128)}, u32[]{:S(2)}) %copy-start) | copy-done | bytes 1474584
  4.6 1.2 %shard_map.37 = f32[8,360,128]{2,1,0:T(8,128)} custom-call(f32[32,11520]{1,0:T(8,128)S(1)} %copy-done), custom_call_target="tpu_custom_call" | custom-call | bytes 2949120 | tf_op jit(solution)/shard_map/pallas_call | solution.py:190
  5.8 0.0 collective-permute-done.b
  5.8 5.4 %all-to-all-start = ((f32[8,360,128]{2,1,0:T(8,128)}), f32[8,360,128]{2,1,0:T(8,128)S(1)}, u32[]{:S(2)}, u32[]{:S(2)}) async-start(f32[8,360,128]{2,1,0:T(8,128)} %shard_map.37), calls=%async_computation | async-start | bytes 2949120 | tf_op jit(solution)/shard_map/all_to_all | solution.py:38
  11.2 7.3 %collective-permute-start.1 = (f32[16,128]{1,0:T(8,128)S(1)}, f32[16,128]{1,0:T(8,128)S(1)}, u32[]{:S(2)}, u32[]{:S(2)}) collective-permute-start(f32[16,128]{1,0:T(8,128)S(1)} %shard_map.38.a), channel_id=1, source_target_pairs={{0,128},{1,129},{2,130},{3,131},{4,132},{5,133},{6,134},{7,135},{8... | collective-permute-start | bytes 24584 | tf_op jit(solution)/shard_map/ppermute | solution.py:50
  18.5 1.6 %collective-permute-done.1.b = f32[16,128]{1,0:T(8,128)S(1)} collective-permute-done((f32[16,128]{1,0:T(8,128)S(1)}, f32[16,128]{1,0:T(8,128)S(1)}, u32[]{:S(2)}, u32[]{:S(2)}) %collective-permute-start.1) | collective-permute-done | bytes 8224 | tf_op jit(solution)/shard_map/ppermute | solution.py:50
  20.1 1.0 %collective-permute-start.2 = (f32[32,128]{1,0:T(8,128)S(1)}, f32[32,128]{1,0:T(8,128)S(1)}, u32[]{:S(2)}, u32[]{:S(2)}) collective-permute-start(f32[32,128]{1,0:T(8,128)S(1)} %shard_map.39.refs_0_), channel_id=1, source_target_pairs={{0,32},{1,33},{2,34},{3,35},{4,36},{5,37},{6,38},{7,39},{8,40},{9,... | collective-permute-start | bytes 49160 | tf_op jit(solution)/shard_map/ppermute | solution.py:50
  21.1 3.6 %collective-permute-start.3 = (f32[32,128]{1,0:T(8,128)S(1)}, f32[32,128]{1,0:T(8,128)S(1)}, u32[]{:S(2)}, u32[]{:S(2)}) collective-permute-start(f32[32,128]{1,0:T(8,128)S(1)} %shard_map.39.refs_0_), channel_id=1, source_target_pairs={{0,224},{1,225},{2,226},{3,227},{4,228},{5,229},{6,230},{7,231},{8... | collective-permute-start | bytes 49160 | tf_op jit(solution)/shard_map/ppermute | solution.py:50
  24.7 1.7 %collective-permute-done.2.refs_1_ = f32[32,128]{1,0:T(8,128)S(1)} collective-permute-done((f32[32,128]{1,0:T(8,128)S(1)}, f32[32,128]{1,0:T(8,128)S(1)}, u32[]{:S(2)}, u32[]{:S(2)}) %collective-permute-start.2) | collective-permute-done | bytes 16416 | tf_op jit(solution)/shard_map/ppermute | solution.py:50
  26.4 4.1 %collective-permute-done.4.refs_3_ = f32[32,128]{1,0:T(8,128)S(1)} collective-permute-done((f32[32,128]{1,0:T(8,128)S(1)}, f32[32,128]{1,0:T(8,128)S(1)}, u32[]{:S(2)}, u32[]{:S(2)}) %collective-permute-start.4) | collective-permute-done | bytes 16416 | tf_op jit(solution)/shard_map/ppermute | solution.py:50
  30.6 1.6 %collective-permute-start.5 = (f32[128,128]{1,0:T(8,128)S(1)}, f32[128,128]{1,0:T(8,128)S(1)}, u32[]{:S(2)}, u32[]{:S(2)}) collective-permute-start(f32[128,128]{1,0:T(8,128)S(1)} %shard_map.40.a), channel_id=1, source_target_pairs={{0,2},{1,3},{2,0},{3,1},{4,6},{5,7},{6,4},{7,5},{8,10},{9,11},{10,... | collective-permute-start | bytes 196616 | tf_op jit(solution)/shard_map/ppermute | solution.py:42
  32.1 2.8 %collective-permute-done.5.b = f32[128,128]{1,0:T(8,128)S(1)} collective-permute-done((f32[128,128]{1,0:T(8,128)S(1)}, f32[128,128]{1,0:T(8,128)S(1)}, u32[]{:S(2)}, u32[]{:S(2)}) %collective-permute-start.5) | collective-permute-done | bytes 65568 | tf_op jit(solution)/shard_map/ppermute | solution.py:42
  34.9 0.1 collective-permute-start.6
  35.0 2.2 %collective-permute-start.12 = (f32[256,128]{1,0:T(8,128)S(1)}, f32[256,128]{1,0:T(8,128)S(1)}, u32[]{:S(2)}, u32[]{:S(2)}) collective-permute-start(f32[256,128]{1,0:T(8,128)S(1)} %shard_map.41.amp), channel_id=1, source_target_pairs={{0,8},{1,9},{2,10},{3,11},{4,12},{5,13},{6,14},{7,15},{8,0},{9,1},... | collective-permute-start | bytes 393224 | tf_op jit(solution)/shard_map/ppermute | solution.py:42
  37.2 1.1 %collective-permute-done.6.other = f32[8,360,128]{2,1,0:T(8,128)S(1)} collective-permute-done((f32[8,360,128]{2,1,0:T(8,128)S(1)}, f32[8,360,128]{2,1,0:T(8,128)S(1)}, u32[]{:S(2)}, u32[]{:S(2)}) %collective-permute-start.6) | collective-permute-done | bytes 1474592 | tf_op jit(solution)/shard_map/ppermute | solution.py:46
  38.3 1.7 %shard_map.42 = (f32[360,128]{1,0:T(8,128)S(1)}, f32[360,128]{1,0:T(8,128)S(1)}, bf16[512,1536]{1,0:T(8,128)(2,1)S(1)}, bf16[512,1536]{1,0:T(8,128)(2,1)S(1)}) custom-call(f32[8,360,128]{2,1,0:T(8,128)S(1)} %all-to-all-done.mine, f32[8,360,128]{2,1,0:T(8,128)S(1)} %collective-permute-done.6.other, f32[256,128]{1,0:T(8,128)S(1)} %shard_map.41.amp), custom_call_target="tpu_custom_call" | custom-call | flops 283115520 | bytes 6594560 | tf_op jit(solution)/shard_map/pallas_call | solution.py:190
  40.0 1.5 %collective-permute-start.7 = (f32[360,128]{1,0:T(8,128)S(1)}, f32[360,128]{1,0:T(8,128)S(1)}, u32[]{:S(2)}, u32[]{:S(2)}) collective-permute-start(f32[360,128]{1,0:T(8,128)S(1)} %get-tuple-element.27), channel_id=1, source_target_pairs={{0,2},{1,3},{2,0},{3,1},{4,6},{5,7},{6,4},{7,5},{8,10},{9,11},{10,... | collective-permute-start | bytes 552968 | tf_op jit(solution)/shard_map/ppermute | solution.py:42
  41.5 1.5 %collective-permute-start.8 = (f32[256,128]{1,0:T(8,128)S(1)}, f32[256,128]{1,0:T(8,128)S(1)}, u32[]{:S(2)}, u32[]{:S(2)}) collective-permute-start(f32[256,128]{1,0:T(8,128)S(1)} %shard_map.41.amp), channel_id=1, source_target_pairs={{0,4},{1,5},{2,6},{3,7},{4,8},{5,9},{6,10},{7,11},{8,12},{9,13},{1... | collective-permute-start | bytes 393224 | tf_op jit(solution)/shard_map/ppermute | solution.py:42
  42.9 0.6 collective-permute-start.9
  43.5 1.0 %shard_map.44 = (f32[360,128]{1,0:T(8,128)S(1)}, f32[360,128]{1,0:T(8,128)S(1)}) custom-call(bf16[512,1536]{1,0:T(8,128)(2,1)S(1)} %get-tuple-element.29.v_hi, bf16[512,1536]{1,0:T(8,128)(2,1)S(1)} %get-tuple-element.30.v_lo, f32[256,128]{1,0:T(8,128)S(1)} %collective-permute-done.12.refs_0_), custom_call_target="tpu_custom_call" | custom-call | flops 283115520 | bytes 3645440 | tf_op jit(solution)/shard_map/pallas_call | solution.py:190
  44.5 2.1 %collective-permute-start.13 = (f32[360,128]{1,0:T(8,128)S(1)}, f32[360,128]{1,0:T(8,128)S(1)}, u32[]{:S(2)}, u32[]{:S(2)}) collective-permute-start(f32[360,128]{1,0:T(8,128)S(1)} %get-tuple-element.33), channel_id=1, source_target_pairs={{0,8},{1,9},{2,10},{3,11},{4,12},{5,13},{6,14},{7,15},{8,0},{9,1},... | collective-permute-start | bytes 552968 | tf_op jit(solution)/shard_map/ppermute | solution.py:42
  46.6 1.5 %collective-permute-start.14 = (f32[360,128]{1,0:T(8,128)S(1)}, f32[360,128]{1,0:T(8,128)S(1)}, u32[]{:S(2)}, u32[]{:S(2)}) collective-permute-start(f32[360,128]{1,0:T(8,128)S(1)} %get-tuple-element.34), channel_id=1, source_target_pairs={{0,10},{1,11},{2,8},{3,9},{4,14},{5,15},{6,12},{7,13},{8,2},{9,3},... | collective-permute-start | bytes 552968 | tf_op jit(solution)/shard_map/ppermute | solution.py:42
  48.1 0.9 %shard_map.43 = (f32[360,128]{1,0:T(8,128)S(1)}, f32[360,128]{1,0:T(8,128)S(1)}, f32[360,128]{1,0:T(8,128)S(1)}, f32[360,128]{1,0:T(8,128)S(1)}) custom-call(bf16[512,1536]{1,0:T(8,128)(2,1)S(1)} %get-tuple-element.29.v_hi, bf16[512,1536]{1,0:T(8,128)(2,1)S(1)} %get-tuple-element.30.v_lo, f32[256,128]{1,0:T(8,128)S(1)} %collective-permute-done.8.refs_0_, ...), custom_call_target="tpu_custom_call" | custom-call | flops 566231040 | bytes 4145152 | tf_op jit(solution)/shard_map/pallas_call | solution.py:190
  48.9 1.7 %collective-permute-start.10 = (f32[360,128]{1,0:T(8,128)S(1)}, f32[360,128]{1,0:T(8,128)S(1)}, u32[]{:S(2)}, u32[]{:S(2)}) collective-permute-start(f32[360,128]{1,0:T(8,128)S(1)} %get-tuple-element.31), channel_id=1, source_target_pairs={{0,4},{1,5},{2,6},{3,7},{4,8},{5,9},{6,10},{7,11},{8,12},{9,13},{1... | collective-permute-start | bytes 552968 | tf_op jit(solution)/shard_map/ppermute | solution.py:42
  50.6 1.9 %collective-permute-start.11 = (f32[360,128]{1,0:T(8,128)S(1)}, f32[360,128]{1,0:T(8,128)S(1)}, u32[]{:S(2)}, u32[]{:S(2)}) collective-permute-start(f32[360,128]{1,0:T(8,128)S(1)} %get-tuple-element.32), channel_id=1, source_target_pairs={{0,6},{1,7},{2,4},{3,5},{4,10},{5,11},{6,8},{7,9},{8,14},{9,15},{1... | collective-permute-start | bytes 552968 | tf_op jit(solution)/shard_map/ppermute | solution.py:42
  52.5 2.7 %collective-permute-start.15 = (f32[360,128]{1,0:T(8,128)S(1)}, f32[360,128]{1,0:T(8,128)S(1)}, u32[]{:S(2)}, u32[]{:S(2)}) collective-permute-start(f32[360,128]{1,0:T(8,128)S(1)} %get-tuple-element.35), channel_id=1, source_target_pairs={{0,12},{1,13},{2,14},{3,15},{4,0},{5,1},{6,2},{7,3},{8,4},{9,5},{1... | collective-permute-start | bytes 552968 | tf_op jit(solution)/shard_map/ppermute | solution.py:42
  55.2 4.0 %collective-permute-start.16 = (f32[360,128]{1,0:T(8,128)S(1)}, f32[360,128]{1,0:T(8,128)S(1)}, u32[]{:S(2)}, u32[]{:S(2)}) collective-permute-start(f32[360,128]{1,0:T(8,128)S(1)} %get-tuple-element.36), channel_id=1, source_target_pairs={{0,14},{1,15},{2,12},{3,13},{4,2},{5,3},{6,0},{7,1},{8,6},{9,7},{1... | collective-permute-start | bytes 552968 | tf_op jit(solution)/shard_map/ppermute | solution.py:42
  59.2 2.3 %collective-permute-done.10.refs_2_ = f32[360,128]{1,0:T(8,128)S(1)} collective-permute-done((f32[360,128]{1,0:T(8,128)S(1)}, f32[360,128]{1,0:T(8,128)S(1)}, u32[]{:S(2)}, u32[]{:S(2)}) %collective-permute-start.10) | collective-permute-done | bytes 184352 | tf_op jit(solution)/shard_map/ppermute | solution.py:42
  61.5 2.8 %collective-permute-done.11.refs_3_ = f32[360,128]{1,0:T(8,128)S(1)} collective-permute-done((f32[360,128]{1,0:T(8,128)S(1)}, f32[360,128]{1,0:T(8,128)S(1)}, u32[]{:S(2)}, u32[]{:S(2)}) %collective-permute-start.11) | collective-permute-done | bytes 184352 | tf_op jit(solution)/shard_map/ppermute | solution.py:42
  64.3 2.6 %collective-permute-done.16.refs_7_ = f32[360,128]{1,0:T(8,128)S(1)} collective-permute-done((f32[360,128]{1,0:T(8,128)S(1)}, f32[360,128]{1,0:T(8,128)S(1)}, u32[]{:S(2)}, u32[]{:S(2)}) %collective-permute-start.16) | collective-permute-done | bytes 184352 | tf_op jit(solution)/shard_map/ppermute | solution.py:42
  66.9 1.4 %shard_map.45 = f32[32,11520]{1,0:T(8,128)} custom-call(f32[360,128]{1,0:T(8,128)S(1)} %get-tuple-element.24.refs_0_, f32[360,128]{1,0:T(8,128)S(1)} %collective-permute-done.7.refs_1_, f32[360,128]{1,0:T(8,128)S(1)} %collective-permute-done.10.refs_2_, f32[360,128]{1,0:T(8,128)S(1)} %collective-permute-done.11.refs_3_, ...), custom_call_target="tpu_custom_call" | custom-call | bytes 4423680 | tf_op jit(solution)/shard_map/pallas_call | solution.py:190
  (19 shorter events, 0.1 us)
Async XLA Ops:
  0.0 5.8 %collective-permute-start = (f32[2,512]{1,0:T(2,128)}, f32[2,512]{1,0:T(2,128)S(1)}, u32[]{:S(2)}, u32[]{:S(2)}) collective-permute-start(f32[2,512]{1,0:T(2,128)} %a.1), channel_id=1, source_target_pairs={{0,16},{1,17},{2,18},{3,19},{4,20},{5,21},{6,22},{7,23},{8,24},{9,... | collective-permute-start | bytes 12296 | tf_op jit(solution)/shard_map/ppermute | solution.py:50
  3.2 1.4 %copy-start = (f32[32,11520]{1,0:T(8,128)S(1)}, f32[32,11520]{1,0:T(8,128)}, u32[]{:S(2)}) copy-start(f32[32,11520]{1,0:T(8,128)} %v.1) | copy-start | bytes 4423684
  5.8 5.4 %copy-start.2 = (f32[2,512]{1,0:T(2,128)S(1)}, f32[2,512]{1,0:T(2,128)}, u32[]{:S(2)}) copy-start(f32[2,512]{1,0:T(2,128)} %a.1) | copy-start | bytes 12292
  5.8 29.1 %all-to-all-start = ((f32[8,360,128]{2,1,0:T(8,128)}), f32[8,360,128]{2,1,0:T(8,128)S(1)}, u32[]{:S(2)}, u32[]{:S(2)}) async-start(f32[8,360,128]{2,1,0:T(8,128)} %shard_map.37), calls=%async_computation | async-start | bytes 2949120 | tf_op jit(solution)/shard_map/all_to_all | solution.py:38
  11.2 8.9 %collective-permute-start.1 = (f32[16,128]{1,0:T(8,128)S(1)}, f32[16,128]{1,0:T(8,128)S(1)}, u32[]{:S(2)}, u32[]{:S(2)}) collective-permute-start(f32[16,128]{1,0:T(8,128)S(1)} %shard_map.38.a), channel_id=1, source_target_pairs={{0,128},{1,129},{2,130},{3,131},{4,132},{5,133},{6,134},{7,135},{8... | collective-permute-start | bytes 24584 | tf_op jit(solution)/shard_map/ppermute | solution.py:50
  20.1 6.3 %collective-permute-start.2 = (f32[32,128]{1,0:T(8,128)S(1)}, f32[32,128]{1,0:T(8,128)S(1)}, u32[]{:S(2)}, u32[]{:S(2)}) collective-permute-start(f32[32,128]{1,0:T(8,128)S(1)} %shard_map.39.refs_0_), channel_id=1, source_target_pairs={{0,32},{1,33},{2,34},{3,35},{4,36},{5,37},{6,38},{7,39},{8,40},{9,... | collective-permute-start | bytes 49160 | tf_op jit(solution)/shard_map/ppermute | solution.py:50
  21.1 5.3 %collective-permute-start.3 = (f32[32,128]{1,0:T(8,128)S(1)}, f32[32,128]{1,0:T(8,128)S(1)}, u32[]{:S(2)}, u32[]{:S(2)}) collective-permute-start(f32[32,128]{1,0:T(8,128)S(1)} %shard_map.39.refs_0_), channel_id=1, source_target_pairs={{0,224},{1,225},{2,226},{3,227},{4,228},{5,229},{6,230},{7,231},{8... | collective-permute-start | bytes 49160 | tf_op jit(solution)/shard_map/ppermute | solution.py:50
  24.7 5.8 %collective-permute-start.4 = (f32[32,128]{1,0:T(8,128)S(1)}, f32[32,128]{1,0:T(8,128)S(1)}, u32[]{:S(2)}, u32[]{:S(2)}) collective-permute-start(f32[32,128]{1,0:T(8,128)S(1)} %shard_map.39.refs_0_), channel_id=1, source_target_pairs={{0,64},{1,193},{2,66},{3,195},{4,68},{5,197},{6,70},{7,199},{8,72}... | collective-permute-start | bytes 49160 | tf_op jit(solution)/shard_map/ppermute | solution.py:50
  30.6 4.4 %collective-permute-start.5 = (f32[128,128]{1,0:T(8,128)S(1)}, f32[128,128]{1,0:T(8,128)S(1)}, u32[]{:S(2)}, u32[]{:S(2)}) collective-permute-start(f32[128,128]{1,0:T(8,128)S(1)} %shard_map.40.a), channel_id=1, source_target_pairs={{0,2},{1,3},{2,0},{3,1},{4,6},{5,7},{6,4},{7,5},{8,10},{9,11},{10,... | collective-permute-start | bytes 196616 | tf_op jit(solution)/shard_map/ppermute | solution.py:42
  34.9 3.4 %collective-permute-start.6 = (f32[8,360,128]{2,1,0:T(8,128)S(1)}, f32[8,360,128]{2,1,0:T(8,128)S(1)}, u32[]{:S(2)}, u32[]{:S(2)}) collective-permute-start(f32[8,360,128]{2,1,0:T(8,128)S(1)} %all-to-all-done.mine), channel_id=1, source_target_pairs={{0,1},{1,0},{2,3},{3,2},{4,5},{5,4},{6,7},{7,6},{8,9},{9,8},{10,11... | collective-permute-start | bytes 4423688 | tf_op jit(solution)/shard_map/ppermute | solution.py:46
  35.0 8.5 %collective-permute-start.12 = (f32[256,128]{1,0:T(8,128)S(1)}, f32[256,128]{1,0:T(8,128)S(1)}, u32[]{:S(2)}, u32[]{:S(2)}) collective-permute-start(f32[256,128]{1,0:T(8,128)S(1)} %shard_map.41.amp), channel_id=1, source_target_pairs={{0,8},{1,9},{2,10},{3,11},{4,12},{5,13},{6,14},{7,15},{8,0},{9,1},... | collective-permute-start | bytes 393224 | tf_op jit(solution)/shard_map/ppermute | solution.py:42
  40.0 8.1 %collective-permute-start.7 = (f32[360,128]{1,0:T(8,128)S(1)}, f32[360,128]{1,0:T(8,128)S(1)}, u32[]{:S(2)}, u32[]{:S(2)}) collective-permute-start(f32[360,128]{1,0:T(8,128)S(1)} %get-tuple-element.27), channel_id=1, source_target_pairs={{0,2},{1,3},{2,0},{3,1},{4,6},{5,7},{6,4},{7,5},{8,10},{9,11},{10,... | collective-permute-start | bytes 552968 | tf_op jit(solution)/shard_map/ppermute | solution.py:42
  41.5 6.6 %collective-permute-start.8 = (f32[256,128]{1,0:T(8,128)S(1)}, f32[256,128]{1,0:T(8,128)S(1)}, u32[]{:S(2)}, u32[]{:S(2)}) collective-permute-start(f32[256,128]{1,0:T(8,128)S(1)} %shard_map.41.amp), channel_id=1, source_target_pairs={{0,4},{1,5},{2,6},{3,7},{4,8},{5,9},{6,10},{7,11},{8,12},{9,13},{1... | collective-permute-start | bytes 393224 | tf_op jit(solution)/shard_map/ppermute | solution.py:42
  42.9 5.1 %collective-permute-start.9 = (f32[256,128]{1,0:T(8,128)S(1)}, f32[256,128]{1,0:T(8,128)S(1)}, u32[]{:S(2)}, u32[]{:S(2)}) collective-permute-start(f32[256,128]{1,0:T(8,128)S(1)} %shard_map.41.amp), channel_id=1, source_target_pairs={{0,12},{1,13},{2,14},{3,15},{4,0},{5,1},{6,2},{7,3},{8,4},{9,5},{1... | collective-permute-start | bytes 393224 | tf_op jit(solution)/shard_map/ppermute | solution.py:42
  44.5 10.7 %collective-permute-start.13 = (f32[360,128]{1,0:T(8,128)S(1)}, f32[360,128]{1,0:T(8,128)S(1)}, u32[]{:S(2)}, u32[]{:S(2)}) collective-permute-start(f32[360,128]{1,0:T(8,128)S(1)} %get-tuple-element.33), channel_id=1, source_target_pairs={{0,8},{1,9},{2,10},{3,11},{4,12},{5,13},{6,14},{7,15},{8,0},{9,1},... | collective-permute-start | bytes 552968 | tf_op jit(solution)/shard_map/ppermute | solution.py:42
  46.6 20.3 %copy-start.1 = (f32[32,11520]{1,0:T(8,128)S(1)}, f32[32,11520]{1,0:T(8,128)}, u32[]{:S(2)}) copy-start(f32[32,11520]{1,0:T(8,128)} %refs_8_.1) | copy-start | bytes 4423684
  46.6 12.7 %collective-permute-start.14 = (f32[360,128]{1,0:T(8,128)S(1)}, f32[360,128]{1,0:T(8,128)S(1)}, u32[]{:S(2)}, u32[]{:S(2)}) collective-permute-start(f32[360,128]{1,0:T(8,128)S(1)} %get-tuple-element.34), channel_id=1, source_target_pairs={{0,10},{1,11},{2,8},{3,9},{4,14},{5,15},{6,12},{7,13},{8,2},{9,3},... | collective-permute-start | bytes 552968 | tf_op jit(solution)/shard_map/ppermute | solution.py:42
  48.9 12.6 %collective-permute-start.10 = (f32[360,128]{1,0:T(8,128)S(1)}, f32[360,128]{1,0:T(8,128)S(1)}, u32[]{:S(2)}, u32[]{:S(2)}) collective-permute-start(f32[360,128]{1,0:T(8,128)S(1)} %get-tuple-element.31), channel_id=1, source_target_pairs={{0,4},{1,5},{2,6},{3,7},{4,8},{5,9},{6,10},{7,11},{8,12},{9,13},{1... | collective-permute-start | bytes 552968 | tf_op jit(solution)/shard_map/ppermute | solution.py:42
  50.6 13.7 %collective-permute-start.11 = (f32[360,128]{1,0:T(8,128)S(1)}, f32[360,128]{1,0:T(8,128)S(1)}, u32[]{:S(2)}, u32[]{:S(2)}) collective-permute-start(f32[360,128]{1,0:T(8,128)S(1)} %get-tuple-element.32), channel_id=1, source_target_pairs={{0,6},{1,7},{2,4},{3,5},{4,10},{5,11},{6,8},{7,9},{8,14},{9,15},{1... | collective-permute-start | bytes 552968 | tf_op jit(solution)/shard_map/ppermute | solution.py:42
  52.5 11.8 %collective-permute-start.15 = (f32[360,128]{1,0:T(8,128)S(1)}, f32[360,128]{1,0:T(8,128)S(1)}, u32[]{:S(2)}, u32[]{:S(2)}) collective-permute-start(f32[360,128]{1,0:T(8,128)S(1)} %get-tuple-element.35), channel_id=1, source_target_pairs={{0,12},{1,13},{2,14},{3,15},{4,0},{5,1},{6,2},{7,3},{8,4},{9,5},{1... | collective-permute-start | bytes 552968 | tf_op jit(solution)/shard_map/ppermute | solution.py:42
  55.2 11.7 %collective-permute-start.16 = (f32[360,128]{1,0:T(8,128)S(1)}, f32[360,128]{1,0:T(8,128)S(1)}, u32[]{:S(2)}, u32[]{:S(2)}) collective-permute-start(f32[360,128]{1,0:T(8,128)S(1)} %get-tuple-element.36), channel_id=1, source_target_pairs={{0,14},{1,15},{2,12},{3,13},{4,2},{5,3},{6,0},{7,1},{8,6},{9,7},{1... | collective-permute-start | bytes 552968 | tf_op jit(solution)/shard_map/ppermute | solution.py:42

commit v4 on v3

--- a/solution.py
+++ b/solution.py
@@ -166,23 +166,52 @@
     return 2 * ((x + 4 + sign * dx) % 4) + (y + dy) % 2
 
 
-def add_rel_kernel(*refs):
-    msgs, previous, out = refs[:8], refs[8], refs[9]
+WIDE = TILES * LANES
+EARLY = [0, 1, 4, 5]
+LATE = [2, 3, 6, 7]
+
+
+def narrow_columns(msgs, offsets, start):
     group = lane_group()
-    narrow = [[jnp.zeros((8, LANES), jnp.float32) for _ in range(4)] for _ in range(2)]
-    for o in range(8):
+    parts = [[start[8 * g : 8 * g + 8, j * LANES : (j + 1) * LANES] for g in range(4)] for j in range(2)]
+    for o, msg in zip(offsets, msgs):
+        q = chip(o, -1, True)
+        folded = msg[TILES * ROWS :, :]
+        for g in range(4):
+            part = pltpu.roll(folded, (ROWS * (q % 4 + 4 - g)) % LANES, 1)
+            for j in range(2):
+                parts[j][g] = parts[j][g] + jnp.where(group + 4 * j == q, part, 0.0)
+    return [jnp.concatenate(p, axis=0) for p in parts]
+
+
+def add_early_kernel(*refs):
+    msgs, previous, out, narrow = refs[:4], refs[4], refs[5], refs[6]
+    for o, msg in zip(EARLY, msgs):
         q = chip(o, -1, True)
         for t in range(TILES):
             at = pl.ds(pl.multiple_of((q * TILES + t) * LANES, LANES), LANES)
-            out[:, at] = previous[:, at] + msgs[o][t * ROWS : (t + 1) * ROWS, :]
-        folded = msgs[o][TILES * ROWS :, :]
-        for g in range(4):
-            part = pltpu.roll(folded, (ROWS * (q % 4 + 4 - g)) % LANES, 1)
-            for j in range(2):
-                narrow[j][g] = jnp.where(group + 4 * j == q, part, narrow[j][g])
-    for j in range(2):
-        at = slice(SPLIT + j * LANES, SPLIT + (j + 1) * LANES)
-        out[:, at] = previous[:, at] + jnp.concatenate(narrow[j], axis=0)
+            out[:, at] = previous[:, at] + msg[t * ROWS : (t + 1) * ROWS, :]
+    for j, value in enumerate(narrow_columns(msgs, EARLY, previous[:, SPLIT:])):
+        narrow[:, j * LANES : (j + 1) * LANES] = value
+
+
+def add_late_kernel(*refs):
+    msgs, previous, narrow, _, out, blocks, last, sems = refs[:4], *refs[4:11]
+    copies = []
+    for n, (o, msg) in enumerate(zip(LATE, msgs)):
+        start = chip(o, -1, True) * WIDE
+        for t in range(TILES):
+            at = pl.ds(pl.multiple_of(start + t * LANES, LANES), LANES)
+            blocks[n, :, t * LANES : (t + 1) * LANES] = previous[:, at] + msg[t * ROWS : (t + 1) * ROWS, :]
+        at = pl.ds(pl.multiple_of(start, LANES), WIDE)
+        copies.append(pltpu.make_async_copy(blocks.at[n], out.at[:, at], sems.at[n]))
+        copies[-1].start()
+    for j, value in enumerate(narrow_columns(msgs, LATE, narrow[...])):
+        last[:, j * LANES : (j + 1) * LANES] = value
+    copies.append(pltpu.make_async_copy(last, out.at[:, pl.ds(SPLIT, 2 * LANES)], sems.at[4]))
+    copies[-1].start()
+    for copy in copies:
+        copy.wait()
 
 
 def call(kernel, outs, args, flops=0, scratch=(), limit=16):
@@ -236,7 +265,24 @@
         for j, dx in enumerate(group):
             for dy in range(2):
                 back[(4 - dx, dy)] = to_chip(out[2 * j + dy], 4 - dx, dy)
-    return call(add_rel_kernel, [f32(*previous.shape)], [back[o] for o in OFFSETS] + [previous])[0]
+    whole, narrow = f32(*previous.shape), f32(ROWS, 2 * LANES)
+    early = [back[OFFSETS[o]] for o in EARLY] + [previous]
+    partial, narrow = call(add_early_kernel, [whole, narrow], early)
+    vmem, hbm = pl.BlockSpec(memory_space=pltpu.VMEM), pl.BlockSpec(memory_space=pl.ANY)
+    return pl.pallas_call(
+        add_late_kernel,
+        out_shape=whole,
+        in_specs=[vmem] * 6 + [hbm],
+        out_specs=hbm,
+        input_output_aliases={6: 0},
+        scratch_shapes=[
+            pltpu.VMEM((4, ROWS, WIDE), jnp.float32),
+            pltpu.VMEM((ROWS, 2 * LANES), jnp.float32),
+            pltpu.SemaphoreType.DMA((5,)),
+        ],
+        compiler_params=pltpu.CompilerParams(vmem_limit_bytes=16 * MIB),
+        cost_estimate=pl.CostEstimate(flops=0, bytes_accessed=3 * 4 * ROWS * 4 * WIDE, transcendentals=0),
+    )(*[back[OFFSETS[o]] for o in LATE], previous, narrow, partial)
 
 
 def solution(mesh):

time: 68.5 us -> 68.1 us (level)
  waiting for transfers between devices: 19.1 us -> 17.8 us
  Pallas kernels: 6.19 us -> 7.03 us
    ppermute x11, waiting for transfers between devices: 10.5 us -> 9.25 us  [to_chip(): return lax.ppermute(a, 'col', cols(lambda x, y, k: (x + dx, y + dy, k)))]
    pallas_call x0 -> x1, Pallas kernels: none -> 1.03 us  [body(): pl.pallas_call(add_late_kernel, out_shape=whole, in_specs=[vmem] * 6 + [h...]
  transfers between devices with their start and end apart: 18 -> 18, of which waited for: 8 -> 8; matrix products, arithmetic and copies ran while one was open for 0% -> 0% of each run, Pallas kernels for 7% -> 9%
where the time goes in v4:
time: 68.1 us; the launch traced here: 68 us
  starting transfers between devices  41.7 us (61%)
  waiting for transfers between devices  17.8 us (26%)
  Pallas kernels  7.03 us (10%)
  local copies, waits for them, and re-layouts  1.38 us (2%)
    ppermute x11, starting transfers between devices, to_chip(): return lax.ppermute(a, 'col', cols(lambda x, y, k: (x + dx, y + dy, k)))  21.1 us
    ppermute x5, starting transfers between devices, over_rows(): return lax.ppermute(a, ('row', 'col'), rows(f))  15.1 us
    ppermute x11, waiting for transfers between devices, to_chip(): return lax.ppermute(a, 'col', cols(lambda x, y, k: (x + dx, y + dy, k)))  9.25 us
    ppermute x5, waiting for transfers between devices, over_rows(): return lax.ppermute(a, ('row', 'col'), rows(f))  7.48 us
    pallas_call x9, Pallas kernels, call(): pl.pallas_call(kernel, out_shape=outs, in_specs=[pl.BlockSpec(memory_spac...  5.99 us
    all_to_all x1, starting transfers between devices, over_chips(): lax.all_to_all(a, 'col', 0, 0, tiled=True, axis_index_groups=OVER_CHIPS)  5.38 us
    unnamed x6, local copies, waits for them, and re-layouts  1.38 us
  transfers between devices with their start and end apart: 18, of which 8 were waited for; matrix products, arithmetic and copies ran while one was open for 0% of the time, Pallas kernels for 9%

profile of v4, /device:TPU:2, one launch (start us, length us, event | category | flops | bytes accessed | tf_op | source)
XLA Modules:
  0.0 68.0 jit_solution(2430952974062572444)
XLA Ops:
  0.0 3.2 %collective-permute-start = (f32[2,512]{1,0:T(2,128)}, f32[2,512]{1,0:T(2,128)S(1)}, u32[]{:S(2)}, u32[]{:S(2)}) collective-permute-start(f32[2,512]{1,0:T(2,128)} %a.1), channel_id=1, source_target_pairs={{0,16},{1,17},{2,18},{3,19},{4,20},{5,21},{6,22},{7,23},{8,24},{9,... | collective-permute-start | bytes 12296 | tf_op jit(solution)/shard_map/ppermute | solution.py:50
  3.2 1.4 %copy-done.1 = f32[32,11520]{1,0:T(8,128)S(1)} copy-done((f32[32,11520]{1,0:T(8,128)S(1)}, f32[32,11520]{1,0:T(8,128)}, u32[]{:S(2)}) %copy-start.1) | copy-done | bytes 1474584
  4.6 1.2 %shard_map.37 = f32[8,360,128]{2,1,0:T(8,128)} custom-call(f32[32,11520]{1,0:T(8,128)S(1)} %copy-done.1), custom_call_target="tpu_custom_call" | custom-call | bytes 2949120 | tf_op jit(solution)/shard_map/pallas_call | solution.py:219
  5.8 5.4 %all-to-all-start = ((f32[8,360,128]{2,1,0:T(8,128)}), f32[8,360,128]{2,1,0:T(8,128)S(1)}, u32[]{:S(2)}, u32[]{:S(2)}) async-start(f32[8,360,128]{2,1,0:T(8,128)} %shard_map.37), calls=%async_computation | async-start | bytes 2949120 | tf_op jit(solution)/shard_map/all_to_all | solution.py:38
  11.2 7.3 %collective-permute-start.1 = (f32[16,128]{1,0:T(8,128)S(1)}, f32[16,128]{1,0:T(8,128)S(1)}, u32[]{:S(2)}, u32[]{:S(2)}) collective-permute-start(f32[16,128]{1,0:T(8,128)S(1)} %shard_map.38.a), channel_id=1, source_target_pairs={{0,128},{1,129},{2,130},{3,131},{4,132},{5,133},{6,134},{7,135},{8... | collective-permute-start | bytes 24584 | tf_op jit(solution)/shard_map/ppermute | solution.py:50
  18.5 1.6 %collective-permute-done.1.b = f32[16,128]{1,0:T(8,128)S(1)} collective-permute-done((f32[16,128]{1,0:T(8,128)S(1)}, f32[16,128]{1,0:T(8,128)S(1)}, u32[]{:S(2)}, u32[]{:S(2)}) %collective-permute-start.1) | collective-permute-done | bytes 8224 | tf_op jit(solution)/shard_map/ppermute | solution.py:50
  20.1 1.0 %collective-permute-start.2 = (f32[32,128]{1,0:T(8,128)S(1)}, f32[32,128]{1,0:T(8,128)S(1)}, u32[]{:S(2)}, u32[]{:S(2)}) collective-permute-start(f32[32,128]{1,0:T(8,128)S(1)} %shard_map.39.refs_0_), channel_id=1, source_target_pairs={{0,32},{1,33},{2,34},{3,35},{4,36},{5,37},{6,38},{7,39},{8,40},{9,... | collective-permute-start | bytes 49160 | tf_op jit(solution)/shard_map/ppermute | solution.py:50
  21.1 3.6 %collective-permute-start.3 = (f32[32,128]{1,0:T(8,128)S(1)}, f32[32,128]{1,0:T(8,128)S(1)}, u32[]{:S(2)}, u32[]{:S(2)}) collective-permute-start(f32[32,128]{1,0:T(8,128)S(1)} %shard_map.39.refs_0_), channel_id=1, source_target_pairs={{0,224},{1,225},{2,226},{3,227},{4,228},{5,229},{6,230},{7,231},{8... | collective-permute-start | bytes 49160 | tf_op jit(solution)/shard_map/ppermute | solution.py:50
  24.7 1.7 %collective-permute-done.2.refs_1_ = f32[32,128]{1,0:T(8,128)S(1)} collective-permute-done((f32[32,128]{1,0:T(8,128)S(1)}, f32[32,128]{1,0:T(8,128)S(1)}, u32[]{:S(2)}, u32[]{:S(2)}) %collective-permute-start.2) | collective-permute-done | bytes 16416 | tf_op jit(solution)/shard_map/ppermute | solution.py:50
  26.4 4.1 %collective-permute-done.4.refs_3_ = f32[32,128]{1,0:T(8,128)S(1)} collective-permute-done((f32[32,128]{1,0:T(8,128)S(1)}, f32[32,128]{1,0:T(8,128)S(1)}, u32[]{:S(2)}, u32[]{:S(2)}) %collective-permute-start.4) | collective-permute-done | bytes 16416 | tf_op jit(solution)/shard_map/ppermute | solution.py:50
  30.6 1.6 %collective-permute-start.5 = (f32[128,128]{1,0:T(8,128)S(1)}, f32[128,128]{1,0:T(8,128)S(1)}, u32[]{:S(2)}, u32[]{:S(2)}) collective-permute-start(f32[128,128]{1,0:T(8,128)S(1)} %shard_map.40.a), channel_id=1, source_target_pairs={{0,2},{1,3},{2,0},{3,1},{4,6},{5,7},{6,4},{7,5},{8,10},{9,11},{10,... | collective-permute-start | bytes 196616 | tf_op jit(solution)/shard_map/ppermute | solution.py:42
  32.1 2.8 %collective-permute-done.5.b = f32[128,128]{1,0:T(8,128)S(1)} collective-permute-done((f32[128,128]{1,0:T(8,128)S(1)}, f32[128,128]{1,0:T(8,128)S(1)}, u32[]{:S(2)}, u32[]{:S(2)}) %collective-permute-start.5) | collective-permute-done | bytes 65568 | tf_op jit(solution)/shard_map/ppermute | solution.py:42
  34.9 0.1 collective-permute-start.6
  35.0 2.2 %collective-permute-start.14 = (f32[256,128]{1,0:T(8,128)S(1)}, f32[256,128]{1,0:T(8,128)S(1)}, u32[]{:S(2)}, u32[]{:S(2)}) collective-permute-start(f32[256,128]{1,0:T(8,128)S(1)} %shard_map.41.amp), channel_id=1, source_target_pairs={{0,8},{1,9},{2,10},{3,11},{4,12},{5,13},{6,14},{7,15},{8,0},{9,1},... | collective-permute-start | bytes 393224 | tf_op jit(solution)/shard_map/ppermute | solution.py:42
  37.2 1.1 %collective-permute-done.6.other = f32[8,360,128]{2,1,0:T(8,128)S(1)} collective-permute-done((f32[8,360,128]{2,1,0:T(8,128)S(1)}, f32[8,360,128]{2,1,0:T(8,128)S(1)}, u32[]{:S(2)}, u32[]{:S(2)}) %collective-permute-start.6) | collective-permute-done | bytes 1474592 | tf_op jit(solution)/shard_map/ppermute | solution.py:46
  38.3 1.7 %shard_map.42 = (f32[360,128]{1,0:T(8,128)S(1)}, f32[360,128]{1,0:T(8,128)S(1)}, bf16[512,1536]{1,0:T(8,128)(2,1)S(1)}, bf16[512,1536]{1,0:T(8,128)(2,1)S(1)}) custom-call(f32[8,360,128]{2,1,0:T(8,128)S(1)} %all-to-all-done.mine, f32[8,360,128]{2,1,0:T(8,128)S(1)} %collective-permute-done.6.other, f32[256,128]{1,0:T(8,128)S(1)} %shard_map.41.amp), custom_call_target="tpu_custom_call" | custom-call | flops 283115520 | bytes 6594560 | tf_op jit(solution)/shard_map/pallas_call | solution.py:219
  40.0 1.5 %collective-permute-start.7 = (f32[360,128]{1,0:T(8,128)S(1)}, f32[360,128]{1,0:T(8,128)S(1)}, u32[]{:S(2)}, u32[]{:S(2)}) collective-permute-start(f32[360,128]{1,0:T(8,128)S(1)} %get-tuple-element.28), channel_id=1, source_target_pairs={{0,2},{1,3},{2,0},{3,1},{4,6},{5,7},{6,4},{7,5},{8,10},{9,11},{10,... | collective-permute-start | bytes 552968 | tf_op jit(solution)/shard_map/ppermute | solution.py:42
  41.5 1.5 %collective-permute-start.8 = (f32[256,128]{1,0:T(8,128)S(1)}, f32[256,128]{1,0:T(8,128)S(1)}, u32[]{:S(2)}, u32[]{:S(2)}) collective-permute-start(f32[256,128]{1,0:T(8,128)S(1)} %shard_map.41.amp), channel_id=1, source_target_pairs={{0,4},{1,5},{2,6},{3,7},{4,8},{5,9},{6,10},{7,11},{8,12},{9,13},{1... | collective-permute-start | bytes 393224 | tf_op jit(solution)/shard_map/ppermute | solution.py:42
  42.9 0.6 collective-permute-start.9
  43.5 1.0 %shard_map.44 = (f32[360,128]{1,0:T(8,128)S(1)}, f32[360,128]{1,0:T(8,128)S(1)}) custom-call(bf16[512,1536]{1,0:T(8,128)(2,1)S(1)} %get-tuple-element.29.v_hi, bf16[512,1536]{1,0:T(8,128)(2,1)S(1)} %get-tuple-element.30.v_lo, f32[256,128]{1,0:T(8,128)S(1)} %collective-permute-done.14.refs_0_), custom_call_target="tpu_custom_call" | custom-call | flops 283115520 | bytes 3645440 | tf_op jit(solution)/shard_map/pallas_call | solution.py:219
  44.5 2.1 %collective-permute-start.15 = (f32[360,128]{1,0:T(8,128)S(1)}, f32[360,128]{1,0:T(8,128)S(1)}, u32[]{:S(2)}, u32[]{:S(2)}) collective-permute-start(f32[360,128]{1,0:T(8,128)S(1)} %get-tuple-element.37), channel_id=1, source_target_pairs={{0,8},{1,9},{2,10},{3,11},{4,12},{5,13},{6,14},{7,15},{8,0},{9,1},... | collective-permute-start | bytes 552968 | tf_op jit(solution)/shard_map/ppermute | solution.py:42
  46.6 1.5 %collective-permute-start.16 = (f32[360,128]{1,0:T(8,128)S(1)}, f32[360,128]{1,0:T(8,128)S(1)}, u32[]{:S(2)}, u32[]{:S(2)}) collective-permute-start(f32[360,128]{1,0:T(8,128)S(1)} %get-tuple-element.38), channel_id=1, source_target_pairs={{0,10},{1,11},{2,8},{3,9},{4,14},{5,15},{6,12},{7,13},{8,2},{9,3},... | collective-permute-start | bytes 552968 | tf_op jit(solution)/shard_map/ppermute | solution.py:42
  48.1 0.9 %shard_map.43 = (f32[360,128]{1,0:T(8,128)S(1)}, f32[360,128]{1,0:T(8,128)S(1)}, f32[360,128]{1,0:T(8,128)S(1)}, f32[360,128]{1,0:T(8,128)S(1)}) custom-call(bf16[512,1536]{1,0:T(8,128)(2,1)S(1)} %get-tuple-element.29.v_hi, bf16[512,1536]{1,0:T(8,128)(2,1)S(1)} %get-tuple-element.30.v_lo, f32[256,128]{1,0:T(8,128)S(1)} %collective-permute-done.8.refs_0_, ...), custom_call_target="tpu_custom_call" | custom-call | flops 566231040 | bytes 4145152 | tf_op jit(solution)/shard_map/pallas_call | solution.py:219
  48.9 1.7 %collective-permute-start.10 = (f32[360,128]{1,0:T(8,128)S(1)}, f32[360,128]{1,0:T(8,128)S(1)}, u32[]{:S(2)}, u32[]{:S(2)}) collective-permute-start(f32[360,128]{1,0:T(8,128)S(1)} %get-tuple-element.31), channel_id=1, source_target_pairs={{0,4},{1,5},{2,6},{3,7},{4,8},{5,9},{6,10},{7,11},{8,12},{9,13},{1... | collective-permute-start | bytes 552968 | tf_op jit(solution)/shard_map/ppermute | solution.py:42
  50.6 1.9 %collective-permute-start.11 = (f32[360,128]{1,0:T(8,128)S(1)}, f32[360,128]{1,0:T(8,128)S(1)}, u32[]{:S(2)}, u32[]{:S(2)}) collective-permute-start(f32[360,128]{1,0:T(8,128)S(1)} %get-tuple-element.32), channel_id=1, source_target_pairs={{0,6},{1,7},{2,4},{3,5},{4,10},{5,11},{6,8},{7,9},{8,14},{9,15},{1... | collective-permute-start | bytes 552968 | tf_op jit(solution)/shard_map/ppermute | solution.py:42
  52.5 2.7 %collective-permute-start.12 = (f32[360,128]{1,0:T(8,128)S(1)}, f32[360,128]{1,0:T(8,128)S(1)}, u32[]{:S(2)}, u32[]{:S(2)}) collective-permute-start(f32[360,128]{1,0:T(8,128)S(1)} %get-tuple-element.33), channel_id=1, source_target_pairs={{0,12},{1,13},{2,14},{3,15},{4,0},{5,1},{6,2},{7,3},{8,4},{9,5},{1... | collective-permute-start | bytes 552968 | tf_op jit(solution)/shard_map/ppermute | solution.py:42
  55.2 4.0 %collective-permute-start.13 = (f32[360,128]{1,0:T(8,128)S(1)}, f32[360,128]{1,0:T(8,128)S(1)}, u32[]{:S(2)}, u32[]{:S(2)}) collective-permute-start(f32[360,128]{1,0:T(8,128)S(1)} %get-tuple-element.34), channel_id=1, source_target_pairs={{0,14},{1,15},{2,12},{3,13},{4,2},{5,3},{6,0},{7,1},{8,6},{9,7},{1... | collective-permute-start | bytes 552968 | tf_op jit(solution)/shard_map/ppermute | solution.py:42
  59.2 1.2 %shard_map.45 = (f32[32,11520]{1,0:T(8,128)}, f32[32,256]{1,0:T(8,128)S(1)}) custom-call(f32[360,128]{1,0:T(8,128)S(1)} %get-tuple-element.35.refs_0_, f32[360,128]{1,0:T(8,128)S(1)} %collective-permute-done.7.refs_1_, f32[360,128]{1,0:T(8,128)S(1)} %collective-permute-done.15.refs_2_, f32[360,128]{1,0:T(8,128)S(1)} %collective-permute-done.16.refs_3_, ...), custom_call_target="tpu_custom_call" | custom-call | bytes 3719168 | tf_op jit(solution)/shard_map/pallas_call | solution.py:219
  60.5 1.1 %collective-permute-done.10.refs_0_ = f32[360,128]{1,0:T(8,128)S(1)} collective-permute-done((f32[360,128]{1,0:T(8,128)S(1)}, f32[360,128]{1,0:T(8,128)S(1)}, u32[]{:S(2)}, u32[]{:S(2)}) %collective-permute-start.10) | collective-permute-done | bytes 184352 | tf_op jit(solution)/shard_map/ppermute | solution.py:42
  61.5 2.8 %collective-permute-done.11.refs_1_ = f32[360,128]{1,0:T(8,128)S(1)} collective-permute-done((f32[360,128]{1,0:T(8,128)S(1)}, f32[360,128]{1,0:T(8,128)S(1)}, u32[]{:S(2)}, u32[]{:S(2)}) %collective-permute-start.11) | collective-permute-done | bytes 184352 | tf_op jit(solution)/shard_map/ppermute | solution.py:42
  64.3 2.6 %collective-permute-done.13.refs_3_ = f32[360,128]{1,0:T(8,128)S(1)} collective-permute-done((f32[360,128]{1,0:T(8,128)S(1)}, f32[360,128]{1,0:T(8,128)S(1)}, u32[]{:S(2)}, u32[]{:S(2)}) %collective-permute-start.13) | collective-permute-done | bytes 184352 | tf_op jit(solution)/shard_map/ppermute | solution.py:42
  66.9 1.0 %shard_map.46 = f32[32,11520]{1,0:T(8,128)} custom-call(f32[360,128]{1,0:T(8,128)S(1)} %collective-permute-done.10.refs_0_, f32[360,128]{1,0:T(8,128)S(1)} %collective-permute-done.11.refs_1_, f32[360,128]{1,0:T(8,128)S(1)} %collective-permute-done.12.refs_2_, f32[360,128]{1,0:T(8,128)S(1)} %collective-permute-done.13.refs_3_, ...), custom_call_target="tpu_custom_call", output_to_operand_aliasing={{}: (6, {})} | custom-call | bytes 2162688 | tf_op jit(solution)/shard_map/pallas_call | solution.py:272
  (20 shorter events, 0.1 us)
Async XLA Ops:
  0.0 5.8 %collective-permute-start = (f32[2,512]{1,0:T(2,128)}, f32[2,512]{1,0:T(2,128)S(1)}, u32[]{:S(2)}, u32[]{:S(2)}) collective-permute-start(f32[2,512]{1,0:T(2,128)} %a.1), channel_id=1, source_target_pairs={{0,16},{1,17},{2,18},{3,19},{4,20},{5,21},{6,22},{7,23},{8,24},{9,... | collective-permute-start | bytes 12296 | tf_op jit(solution)/shard_map/ppermute | solution.py:50
  3.2 1.4 %copy-start.1 = (f32[32,11520]{1,0:T(8,128)S(1)}, f32[32,11520]{1,0:T(8,128)}, u32[]{:S(2)}) copy-start(f32[32,11520]{1,0:T(8,128)} %v.1) | copy-start | bytes 4423684
  5.8 5.4 %copy-start.2 = (f32[2,512]{1,0:T(2,128)S(1)}, f32[2,512]{1,0:T(2,128)}, u32[]{:S(2)}) copy-start(f32[2,512]{1,0:T(2,128)} %a.1) | copy-start | bytes 12292
  5.8 29.1 %all-to-all-start = ((f32[8,360,128]{2,1,0:T(8,128)}), f32[8,360,128]{2,1,0:T(8,128)S(1)}, u32[]{:S(2)}, u32[]{:S(2)}) async-start(f32[8,360,128]{2,1,0:T(8,128)} %shard_map.37), calls=%async_computation | async-start | bytes 2949120 | tf_op jit(solution)/shard_map/all_to_all | solution.py:38
  11.2 8.9 %collective-permute-start.1 = (f32[16,128]{1,0:T(8,128)S(1)}, f32[16,128]{1,0:T(8,128)S(1)}, u32[]{:S(2)}, u32[]{:S(2)}) collective-permute-start(f32[16,128]{1,0:T(8,128)S(1)} %shard_map.38.a), channel_id=1, source_target_pairs={{0,128},{1,129},{2,130},{3,131},{4,132},{5,133},{6,134},{7,135},{8... | collective-permute-start | bytes 24584 | tf_op jit(solution)/shard_map/ppermute | solution.py:50
  20.1 6.3 %collective-permute-start.2 = (f32[32,128]{1,0:T(8,128)S(1)}, f32[32,128]{1,0:T(8,128)S(1)}, u32[]{:S(2)}, u32[]{:S(2)}) collective-permute-start(f32[32,128]{1,0:T(8,128)S(1)} %shard_map.39.refs_0_), channel_id=1, source_target_pairs={{0,32},{1,33},{2,34},{3,35},{4,36},{5,37},{6,38},{7,39},{8,40},{9,... | collective-permute-start | bytes 49160 | tf_op jit(solution)/shard_map/ppermute | solution.py:50
  21.1 5.3 %collective-permute-start.3 = (f32[32,128]{1,0:T(8,128)S(1)}, f32[32,128]{1,0:T(8,128)S(1)}, u32[]{:S(2)}, u32[]{:S(2)}) collective-permute-start(f32[32,128]{1,0:T(8,128)S(1)} %shard_map.39.refs_0_), channel_id=1, source_target_pairs={{0,224},{1,225},{2,226},{3,227},{4,228},{5,229},{6,230},{7,231},{8... | collective-permute-start | bytes 49160 | tf_op jit(solution)/shard_map/ppermute | solution.py:50
  24.7 5.8 %collective-permute-start.4 = (f32[32,128]{1,0:T(8,128)S(1)}, f32[32,128]{1,0:T(8,128)S(1)}, u32[]{:S(2)}, u32[]{:S(2)}) collective-permute-start(f32[32,128]{1,0:T(8,128)S(1)} %shard_map.39.refs_0_), channel_id=1, source_target_pairs={{0,64},{1,193},{2,66},{3,195},{4,68},{5,197},{6,70},{7,199},{8,72}... | collective-permute-start | bytes 49160 | tf_op jit(solution)/shard_map/ppermute | solution.py:50
  30.6 4.4 %collective-permute-start.5 = (f32[128,128]{1,0:T(8,128)S(1)}, f32[128,128]{1,0:T(8,128)S(1)}, u32[]{:S(2)}, u32[]{:S(2)}) collective-permute-start(f32[128,128]{1,0:T(8,128)S(1)} %shard_map.40.a), channel_id=1, source_target_pairs={{0,2},{1,3},{2,0},{3,1},{4,6},{5,7},{6,4},{7,5},{8,10},{9,11},{10,... | collective-permute-start | bytes 196616 | tf_op jit(solution)/shard_map/ppermute | solution.py:42
  34.9 3.4 %collective-permute-start.6 = (f32[8,360,128]{2,1,0:T(8,128)S(1)}, f32[8,360,128]{2,1,0:T(8,128)S(1)}, u32[]{:S(2)}, u32[]{:S(2)}) collective-permute-start(f32[8,360,128]{2,1,0:T(8,128)S(1)} %all-to-all-done.mine), channel_id=1, source_target_pairs={{0,1},{1,0},{2,3},{3,2},{4,5},{5,4},{6,7},{7,6},{8,9},{9,8},{10,11... | collective-permute-start | bytes 4423688 | tf_op jit(solution)/shard_map/ppermute | solution.py:46
  35.0 8.5 %collective-permute-start.14 = (f32[256,128]{1,0:T(8,128)S(1)}, f32[256,128]{1,0:T(8,128)S(1)}, u32[]{:S(2)}, u32[]{:S(2)}) collective-permute-start(f32[256,128]{1,0:T(8,128)S(1)} %shard_map.41.amp), channel_id=1, source_target_pairs={{0,8},{1,9},{2,10},{3,11},{4,12},{5,13},{6,14},{7,15},{8,0},{9,1},... | collective-permute-start | bytes 393224 | tf_op jit(solution)/shard_map/ppermute | solution.py:42
  40.0 8.1 %collective-permute-start.7 = (f32[360,128]{1,0:T(8,128)S(1)}, f32[360,128]{1,0:T(8,128)S(1)}, u32[]{:S(2)}, u32[]{:S(2)}) collective-permute-start(f32[360,128]{1,0:T(8,128)S(1)} %get-tuple-element.28), channel_id=1, source_target_pairs={{0,2},{1,3},{2,0},{3,1},{4,6},{5,7},{6,4},{7,5},{8,10},{9,11},{10,... | collective-permute-start | bytes 552968 | tf_op jit(solution)/shard_map/ppermute | solution.py:42
  41.5 6.6 %collective-permute-start.8 = (f32[256,128]{1,0:T(8,128)S(1)}, f32[256,128]{1,0:T(8,128)S(1)}, u32[]{:S(2)}, u32[]{:S(2)}) collective-permute-start(f32[256,128]{1,0:T(8,128)S(1)} %shard_map.41.amp), channel_id=1, source_target_pairs={{0,4},{1,5},{2,6},{3,7},{4,8},{5,9},{6,10},{7,11},{8,12},{9,13},{1... | collective-permute-start | bytes 393224 | tf_op jit(solution)/shard_map/ppermute | solution.py:42
  42.9 5.1 %collective-permute-start.9 = (f32[256,128]{1,0:T(8,128)S(1)}, f32[256,128]{1,0:T(8,128)S(1)}, u32[]{:S(2)}, u32[]{:S(2)}) collective-permute-start(f32[256,128]{1,0:T(8,128)S(1)} %shard_map.41.amp), channel_id=1, source_target_pairs={{0,12},{1,13},{2,14},{3,15},{4,0},{5,1},{6,2},{7,3},{8,4},{9,5},{1... | collective-permute-start | bytes 393224 | tf_op jit(solution)/shard_map/ppermute | solution.py:42
  44.5 10.7 %collective-permute-start.15 = (f32[360,128]{1,0:T(8,128)S(1)}, f32[360,128]{1,0:T(8,128)S(1)}, u32[]{:S(2)}, u32[]{:S(2)}) collective-permute-start(f32[360,128]{1,0:T(8,128)S(1)} %get-tuple-element.37), channel_id=1, source_target_pairs={{0,8},{1,9},{2,10},{3,11},{4,12},{5,13},{6,14},{7,15},{8,0},{9,1},... | collective-permute-start | bytes 552968 | tf_op jit(solution)/shard_map/ppermute | solution.py:42
  46.6 12.7 %copy-start = (f32[32,11520]{1,0:T(8,128)S(1)}, f32[32,11520]{1,0:T(8,128)}, u32[]{:S(2)}) copy-start(f32[32,11520]{1,0:T(8,128)} %refs_4_.3) | copy-start | bytes 4423684
  46.6 12.7 %collective-permute-start.16 = (f32[360,128]{1,0:T(8,128)S(1)}, f32[360,128]{1,0:T(8,128)S(1)}, u32[]{:S(2)}, u32[]{:S(2)}) collective-permute-start(f32[360,128]{1,0:T(8,128)S(1)} %get-tuple-element.38), channel_id=1, source_target_pairs={{0,10},{1,11},{2,8},{3,9},{4,14},{5,15},{6,12},{7,13},{8,2},{9,3},... | collective-permute-start | bytes 552968 | tf_op jit(solution)/shard_map/ppermute | solution.py:42
  48.9 12.6 %collective-permute-start.10 = (f32[360,128]{1,0:T(8,128)S(1)}, f32[360,128]{1,0:T(8,128)S(1)}, u32[]{:S(2)}, u32[]{:S(2)}) collective-permute-start(f32[360,128]{1,0:T(8,128)S(1)} %get-tuple-element.31), channel_id=1, source_target_pairs={{0,4},{1,5},{2,6},{3,7},{4,8},{5,9},{6,10},{7,11},{8,12},{9,13},{1... | collective-permute-start | bytes 552968 | tf_op jit(solution)/shard_map/ppermute | solution.py:42
  50.6 13.7 %collective-permute-start.11 = (f32[360,128]{1,0:T(8,128)S(1)}, f32[360,128]{1,0:T(8,128)S(1)}, u32[]{:S(2)}, u32[]{:S(2)}) collective-permute-start(f32[360,128]{1,0:T(8,128)S(1)} %get-tuple-element.32), channel_id=1, source_target_pairs={{0,6},{1,7},{2,4},{3,5},{4,10},{5,11},{6,8},{7,9},{8,14},{9,15},{1... | collective-permute-start | bytes 552968 | tf_op jit(solution)/shard_map/ppermute | solution.py:42
  52.5 11.8 %collective-permute-start.12 = (f32[360,128]{1,0:T(8,128)S(1)}, f32[360,128]{1,0:T(8,128)S(1)}, u32[]{:S(2)}, u32[]{:S(2)}) collective-permute-start(f32[360,128]{1,0:T(8,128)S(1)} %get-tuple-element.33), channel_id=1, source_target_pairs={{0,12},{1,13},{2,14},{3,15},{4,0},{5,1},{6,2},{7,3},{8,4},{9,5},{1... | collective-permute-start | bytes 552968 | tf_op jit(solution)/shard_map/ppermute | solution.py:42
  55.2 11.7 %collective-permute-start.13 = (f32[360,128]{1,0:T(8,128)S(1)}, f32[360,128]{1,0:T(8,128)S(1)}, u32[]{:S(2)}, u32[]{:S(2)}) collective-permute-start(f32[360,128]{1,0:T(8,128)S(1)} %get-tuple-element.34), channel_id=1, source_target_pairs={{0,14},{1,15},{2,12},{3,13},{4,2},{5,3},{6,0},{7,1},{8,6},{9,7},{1... | collective-permute-start | bytes 552968 | tf_op jit(solution)/shard_map/ppermute | solution.py:42

commit v5 on v4

--- a/solution.py
+++ b/solution.py
@@ -195,10 +195,9 @@
         narrow[:, j * LANES : (j + 1) * LANES] = value
 
 
-def add_late_kernel(*refs):
-    msgs, previous, narrow, _, out, blocks, last, sems = refs[:4], *refs[4:11]
+def write_blocks(offsets, msgs, previous, out, blocks, sems):
     copies = []
-    for n, (o, msg) in enumerate(zip(LATE, msgs)):
+    for n, (o, msg) in enumerate(zip(offsets, msgs)):
         start = chip(o, -1, True) * WIDE
         for t in range(TILES):
             at = pl.ds(pl.multiple_of(start + t * LANES, LANES), LANES)
@@ -206,12 +205,38 @@
         at = pl.ds(pl.multiple_of(start, LANES), WIDE)
         copies.append(pltpu.make_async_copy(blocks.at[n], out.at[:, at], sems.at[n]))
         copies[-1].start()
+    return copies
+
+
+def add_middle_kernel(m0, m1, previous, _, out, blocks, sems):
+    for copy in write_blocks(LATE[:2], (m0, m1), previous, out, blocks, sems):
+        copy.wait()
+
+
+def add_late_kernel(*refs):
+    msgs, previous, narrow, _, out, blocks, last, sems = refs[:4], *refs[4:11]
+    copies = write_blocks(LATE[2:], msgs[2:], previous, out, blocks, sems)
     for j, value in enumerate(narrow_columns(msgs, LATE, narrow[...])):
         last[:, j * LANES : (j + 1) * LANES] = value
-    copies.append(pltpu.make_async_copy(last, out.at[:, pl.ds(SPLIT, 2 * LANES)], sems.at[4]))
+    copies.append(pltpu.make_async_copy(last, out.at[:, pl.ds(SPLIT, 2 * LANES)], sems.at[2]))
     copies[-1].start()
     for copy in copies:
         copy.wait()
+
+
+def add_in_place(kernel, args, scratch, sems):
+    vmem, hbm = pl.BlockSpec(memory_space=pltpu.VMEM), pl.BlockSpec(memory_space=pl.ANY)
+    n = len(args) - 1
+    return pl.pallas_call(
+        kernel,
+        out_shape=f32(*args[n].shape),
+        in_specs=[vmem] * n + [hbm],
+        out_specs=hbm,
+        input_output_aliases={n: 0},
+        scratch_shapes=[pltpu.VMEM((2, ROWS, WIDE), jnp.float32)] + scratch + [pltpu.SemaphoreType.DMA((sems,))],
+        compiler_params=pltpu.CompilerParams(vmem_limit_bytes=16 * MIB),
+        cost_estimate=pl.CostEstimate(flops=0, bytes_accessed=3 * 2 * ROWS * 4 * WIDE, transcendentals=0),
+    )(*args)
 
 
 def call(kernel, outs, args, flops=0, scratch=(), limit=16):
@@ -268,21 +293,10 @@
     whole, narrow = f32(*previous.shape), f32(ROWS, 2 * LANES)
     early = [back[OFFSETS[o]] for o in EARLY] + [previous]
     partial, narrow = call(add_early_kernel, [whole, narrow], early)
-    vmem, hbm = pl.BlockSpec(memory_space=pltpu.VMEM), pl.BlockSpec(memory_space=pl.ANY)
-    return pl.pallas_call(
-        add_late_kernel,
-        out_shape=whole,
-        in_specs=[vmem] * 6 + [hbm],
-        out_specs=hbm,
-        input_output_aliases={6: 0},
-        scratch_shapes=[
-            pltpu.VMEM((4, ROWS, WIDE), jnp.float32),
-            pltpu.VMEM((ROWS, 2 * LANES), jnp.float32),
-            pltpu.SemaphoreType.DMA((5,)),
-        ],
-        compiler_params=pltpu.CompilerParams(vmem_limit_bytes=16 * MIB),
-        cost_estimate=pl.CostEstimate(flops=0, bytes_accessed=3 * 4 * ROWS * 4 * WIDE, transcendentals=0),
-    )(*[back[OFFSETS[o]] for o in LATE], previous, narrow, partial)
+    late = [back[OFFSETS[o]] for o in LATE]
+    partial = add_in_place(add_middle_kernel, late[:2] + [previous, partial], [], 2)
+    last = pltpu.VMEM((ROWS, 2 * LANES), jnp.float32)
+    return add_in_place(add_late_kernel, late + [previous, narrow, partial], [last], 3)
 
 
 def solution(mesh):

time: 68.1 us -> 68 us (level)
  waiting for transfers between devices: 17.8 us -> 17 us
    ppermute x11, waiting for transfers between devices: 9.25 us -> 8.47 us  [to_chip(): return lax.ppermute(a, 'col', cols(lambda x, y, k: (x + dx, y + dy, k)))]
    pallas_call x1 -> x2, Pallas kernels: 1.03 us -> 1.61 us  [add_in_place(): pl.pallas_call(kernel, out_shape=f32(*args[n].shape), in_specs=[vmem] * n...]
  transfers between devices with their start and end apart: 18 -> 18, of which waited for: 8 -> 8; matrix products, arithmetic and copies ran while one was open for 0% -> 0% of each run, Pallas kernels for 9% -> 10%
where the time goes in v5:
time: 68 us; the launch traced here: 67.8 us
  starting transfers between devices  41.7 us (61%)
  waiting for transfers between devices  17 us (25%)
  Pallas kernels  7.61 us (11%)
  local copies, waits for them, and re-layouts  1.38 us (2%)
    ppermute x11, starting transfers between devices, to_chip(): return lax.ppermute(a, 'col', cols(lambda x, y, k: (x + dx, y + dy, k)))  21.1 us
    ppermute x5, starting transfers between devices, over_rows(): return lax.ppermute(a, ('row', 'col'), rows(f))  15.1 us
    ppermute x11, waiting for transfers between devices, to_chip(): return lax.ppermute(a, 'col', cols(lambda x, y, k: (x + dx, y + dy, k)))  8.47 us
    ppermute x5, waiting for transfers between devices, over_rows(): return lax.ppermute(a, ('row', 'col'), rows(f))  7.48 us
    pallas_call x9, Pallas kernels, call(): pl.pallas_call(kernel, out_shape=outs, in_specs=[pl.BlockSpec(memory_spac...  5.99 us
    all_to_all x1, starting transfers between devices, over_chips(): lax.all_to_all(a, 'col', 0, 0, tiled=True, axis_index_groups=OVER_CHIPS)  5.38 us
    pallas_call x2, Pallas kernels, add_in_place(): pl.pallas_call(kernel, out_shape=f32(*args[n].shape), in_specs=[vmem] * n...  1.61 us
    unnamed x6, local copies, waits for them, and re-layouts  1.38 us
  transfers between devices with their start and end apart: 18, of which 8 were waited for; matrix products, arithmetic and copies ran while one was open for 0% of the time, Pallas kernels for 10%

profile of v5, /device:TPU:2, one launch (start us, length us, event | category | flops | bytes accessed | tf_op | source)
XLA Modules:
  0.0 67.8 jit_solution(17452351087660401752)
XLA Ops:
  0.0 3.2 %collective-permute-start = (f32[2,512]{1,0:T(2,128)}, f32[2,512]{1,0:T(2,128)S(1)}, u32[]{:S(2)}, u32[]{:S(2)}) collective-permute-start(f32[2,512]{1,0:T(2,128)} %a.1), channel_id=1, source_target_pairs={{0,16},{1,17},{2,18},{3,19},{4,20},{5,21},{6,22},{7,23},{8,24},{9,... | collective-permute-start | bytes 12296 | tf_op jit(solution)/shard_map/ppermute | solution.py:50
  3.2 1.4 %copy-done.1 = f32[32,11520]{1,0:T(8,128)S(1)} copy-done((f32[32,11520]{1,0:T(8,128)S(1)}, f32[32,11520]{1,0:T(8,128)}, u32[]{:S(2)}) %copy-start.1) | copy-done | bytes 1474584
  4.6 1.2 %shard_map.37 = f32[8,360,128]{2,1,0:T(8,128)} custom-call(f32[32,11520]{1,0:T(8,128)S(1)} %copy-done.1), custom_call_target="tpu_custom_call" | custom-call | bytes 2949120 | tf_op jit(solution)/shard_map/pallas_call | solution.py:244
  5.8 5.4 %all-to-all-start = ((f32[8,360,128]{2,1,0:T(8,128)}), f32[8,360,128]{2,1,0:T(8,128)S(1)}, u32[]{:S(2)}, u32[]{:S(2)}) async-start(f32[8,360,128]{2,1,0:T(8,128)} %shard_map.37), calls=%async_computation | async-start | bytes 2949120 | tf_op jit(solution)/shard_map/all_to_all | solution.py:38
  11.2 7.3 %collective-permute-start.1 = (f32[16,128]{1,0:T(8,128)S(1)}, f32[16,128]{1,0:T(8,128)S(1)}, u32[]{:S(2)}, u32[]{:S(2)}) collective-permute-start(f32[16,128]{1,0:T(8,128)S(1)} %shard_map.38.a), channel_id=1, source_target_pairs={{0,128},{1,129},{2,130},{3,131},{4,132},{5,133},{6,134},{7,135},{8... | collective-permute-start | bytes 24584 | tf_op jit(solution)/shard_map/ppermute | solution.py:50
  18.5 1.6 %collective-permute-done.1.b = f32[16,128]{1,0:T(8,128)S(1)} collective-permute-done((f32[16,128]{1,0:T(8,128)S(1)}, f32[16,128]{1,0:T(8,128)S(1)}, u32[]{:S(2)}, u32[]{:S(2)}) %collective-permute-start.1) | collective-permute-done | bytes 8224 | tf_op jit(solution)/shard_map/ppermute | solution.py:50
  20.1 1.0 %collective-permute-start.2 = (f32[32,128]{1,0:T(8,128)S(1)}, f32[32,128]{1,0:T(8,128)S(1)}, u32[]{:S(2)}, u32[]{:S(2)}) collective-permute-start(f32[32,128]{1,0:T(8,128)S(1)} %shard_map.39.refs_0_), channel_id=1, source_target_pairs={{0,32},{1,33},{2,34},{3,35},{4,36},{5,37},{6,38},{7,39},{8,40},{9,... | collective-permute-start | bytes 49160 | tf_op jit(solution)/shard_map/ppermute | solution.py:50
  21.1 3.6 %collective-permute-start.3 = (f32[32,128]{1,0:T(8,128)S(1)}, f32[32,128]{1,0:T(8,128)S(1)}, u32[]{:S(2)}, u32[]{:S(2)}) collective-permute-start(f32[32,128]{1,0:T(8,128)S(1)} %shard_map.39.refs_0_), channel_id=1, source_target_pairs={{0,224},{1,225},{2,226},{3,227},{4,228},{5,229},{6,230},{7,231},{8... | collective-permute-start | bytes 49160 | tf_op jit(solution)/shard_map/ppermute | solution.py:50
  24.7 1.7 %collective-permute-done.2.refs_1_ = f32[32,128]{1,0:T(8,128)S(1)} collective-permute-done((f32[32,128]{1,0:T(8,128)S(1)}, f32[32,128]{1,0:T(8,128)S(1)}, u32[]{:S(2)}, u32[]{:S(2)}) %collective-permute-start.2) | collective-permute-done | bytes 16416 | tf_op jit(solution)/shard_map/ppermute | solution.py:50
  26.4 4.1 %collective-permute-done.4.refs_3_ = f32[32,128]{1,0:T(8,128)S(1)} collective-permute-done((f32[32,128]{1,0:T(8,128)S(1)}, f32[32,128]{1,0:T(8,128)S(1)}, u32[]{:S(2)}, u32[]{:S(2)}) %collective-permute-start.4) | collective-permute-done | bytes 16416 | tf_op jit(solution)/shard_map/ppermute | solution.py:50
  30.6 1.6 %collective-permute-start.5 = (f32[128,128]{1,0:T(8,128)S(1)}, f32[128,128]{1,0:T(8,128)S(1)}, u32[]{:S(2)}, u32[]{:S(2)}) collective-permute-start(f32[128,128]{1,0:T(8,128)S(1)} %shard_map.40.a), channel_id=1, source_target_pairs={{0,2},{1,3},{2,0},{3,1},{4,6},{5,7},{6,4},{7,5},{8,10},{9,11},{10,... | collective-permute-start | bytes 196616 | tf_op jit(solution)/shard_map/ppermute | solution.py:42
  32.1 2.8 %collective-permute-done.5.b = f32[128,128]{1,0:T(8,128)S(1)} collective-permute-done((f32[128,128]{1,0:T(8,128)S(1)}, f32[128,128]{1,0:T(8,128)S(1)}, u32[]{:S(2)}, u32[]{:S(2)}) %collective-permute-start.5) | collective-permute-done | bytes 65568 | tf_op jit(solution)/shard_map/ppermute | solution.py:42
  35.0 2.2 %collective-permute-start.14 = (f32[256,128]{1,0:T(8,128)S(1)}, f32[256,128]{1,0:T(8,128)S(1)}, u32[]{:S(2)}, u32[]{:S(2)}) collective-permute-start(f32[256,128]{1,0:T(8,128)S(1)} %shard_map.41.amp), channel_id=1, source_target_pairs={{0,8},{1,9},{2,10},{3,11},{4,12},{5,13},{6,14},{7,15},{8,0},{9,1},... | collective-permute-start | bytes 393224 | tf_op jit(solution)/shard_map/ppermute | solution.py:42
  37.2 1.1 %collective-permute-done.6.other = f32[8,360,128]{2,1,0:T(8,128)S(1)} collective-permute-done((f32[8,360,128]{2,1,0:T(8,128)S(1)}, f32[8,360,128]{2,1,0:T(8,128)S(1)}, u32[]{:S(2)}, u32[]{:S(2)}) %collective-permute-start.6) | collective-permute-done | bytes 1474592 | tf_op jit(solution)/shard_map/ppermute | solution.py:46
  38.3 1.7 %shard_map.42 = (f32[360,128]{1,0:T(8,128)S(1)}, f32[360,128]{1,0:T(8,128)S(1)}, bf16[512,1536]{1,0:T(8,128)(2,1)S(1)}, bf16[512,1536]{1,0:T(8,128)(2,1)S(1)}) custom-call(f32[8,360,128]{2,1,0:T(8,128)S(1)} %all-to-all-done.mine, f32[8,360,128]{2,1,0:T(8,128)S(1)} %collective-permute-done.6.other, f32[256,128]{1,0:T(8,128)S(1)} %shard_map.41.amp), custom_call_target="tpu_custom_call" | custom-call | flops 283115520 | bytes 6594560 | tf_op jit(solution)/shard_map/pallas_call | solution.py:244
  40.0 1.5 %collective-permute-start.7 = (f32[360,128]{1,0:T(8,128)S(1)}, f32[360,128]{1,0:T(8,128)S(1)}, u32[]{:S(2)}, u32[]{:S(2)}) collective-permute-start(f32[360,128]{1,0:T(8,128)S(1)} %get-tuple-element.28), channel_id=1, source_target_pairs={{0,2},{1,3},{2,0},{3,1},{4,6},{5,7},{6,4},{7,5},{8,10},{9,11},{10,... | collective-permute-start | bytes 552968 | tf_op jit(solution)/shard_map/ppermute | solution.py:42
  41.5 1.5 %collective-permute-start.8 = (f32[256,128]{1,0:T(8,128)S(1)}, f32[256,128]{1,0:T(8,128)S(1)}, u32[]{:S(2)}, u32[]{:S(2)}) collective-permute-start(f32[256,128]{1,0:T(8,128)S(1)} %shard_map.41.amp), channel_id=1, source_target_pairs={{0,4},{1,5},{2,6},{3,7},{4,8},{5,9},{6,10},{7,11},{8,12},{9,13},{1... | collective-permute-start | bytes 393224 | tf_op jit(solution)/shard_map/ppermute | solution.py:42
  42.9 0.6 collective-permute-start.9
  43.5 1.0 %shard_map.44 = (f32[360,128]{1,0:T(8,128)S(1)}, f32[360,128]{1,0:T(8,128)S(1)}) custom-call(bf16[512,1536]{1,0:T(8,128)(2,1)S(1)} %get-tuple-element.29.v_hi, bf16[512,1536]{1,0:T(8,128)(2,1)S(1)} %get-tuple-element.30.v_lo, f32[256,128]{1,0:T(8,128)S(1)} %collective-permute-done.14.refs_0_), custom_call_target="tpu_custom_call" | custom-call | flops 283115520 | bytes 3645440 | tf_op jit(solution)/shard_map/pallas_call | solution.py:244
  44.5 2.1 %collective-permute-start.15 = (f32[360,128]{1,0:T(8,128)S(1)}, f32[360,128]{1,0:T(8,128)S(1)}, u32[]{:S(2)}, u32[]{:S(2)}) collective-permute-start(f32[360,128]{1,0:T(8,128)S(1)} %get-tuple-element.37), channel_id=1, source_target_pairs={{0,8},{1,9},{2,10},{3,11},{4,12},{5,13},{6,14},{7,15},{8,0},{9,1},... | collective-permute-start | bytes 552968 | tf_op jit(solution)/shard_map/ppermute | solution.py:42
  46.6 1.5 %collective-permute-start.16 = (f32[360,128]{1,0:T(8,128)S(1)}, f32[360,128]{1,0:T(8,128)S(1)}, u32[]{:S(2)}, u32[]{:S(2)}) collective-permute-start(f32[360,128]{1,0:T(8,128)S(1)} %get-tuple-element.38), channel_id=1, source_target_pairs={{0,10},{1,11},{2,8},{3,9},{4,14},{5,15},{6,12},{7,13},{8,2},{9,3},... | collective-permute-start | bytes 552968 | tf_op jit(solution)/shard_map/ppermute | solution.py:42
  48.1 0.9 %shard_map.43 = (f32[360,128]{1,0:T(8,128)S(1)}, f32[360,128]{1,0:T(8,128)S(1)}, f32[360,128]{1,0:T(8,128)S(1)}, f32[360,128]{1,0:T(8,128)S(1)}) custom-call(bf16[512,1536]{1,0:T(8,128)(2,1)S(1)} %get-tuple-element.29.v_hi, bf16[512,1536]{1,0:T(8,128)(2,1)S(1)} %get-tuple-element.30.v_lo, f32[256,128]{1,0:T(8,128)S(1)} %collective-permute-done.8.refs_0_, ...), custom_call_target="tpu_custom_call" | custom-call | flops 566231040 | bytes 4145152 | tf_op jit(solution)/shard_map/pallas_call | solution.py:244
  48.9 1.7 %collective-permute-start.10 = (f32[360,128]{1,0:T(8,128)S(1)}, f32[360,128]{1,0:T(8,128)S(1)}, u32[]{:S(2)}, u32[]{:S(2)}) collective-permute-start(f32[360,128]{1,0:T(8,128)S(1)} %get-tuple-element.31), channel_id=1, source_target_pairs={{0,4},{1,5},{2,6},{3,7},{4,8},{5,9},{6,10},{7,11},{8,12},{9,13},{1... | collective-permute-start | bytes 552968 | tf_op jit(solution)/shard_map/ppermute | solution.py:42
  50.6 1.9 %collective-permute-start.11 = (f32[360,128]{1,0:T(8,128)S(1)}, f32[360,128]{1,0:T(8,128)S(1)}, u32[]{:S(2)}, u32[]{:S(2)}) collective-permute-start(f32[360,128]{1,0:T(8,128)S(1)} %get-tuple-element.32), channel_id=1, source_target_pairs={{0,6},{1,7},{2,4},{3,5},{4,10},{5,11},{6,8},{7,9},{8,14},{9,15},{1... | collective-permute-start | bytes 552968 | tf_op jit(solution)/shard_map/ppermute | solution.py:42
  52.5 2.7 %collective-permute-start.12 = (f32[360,128]{1,0:T(8,128)S(1)}, f32[360,128]{1,0:T(8,128)S(1)}, u32[]{:S(2)}, u32[]{:S(2)}) collective-permute-start(f32[360,128]{1,0:T(8,128)S(1)} %get-tuple-element.33), channel_id=1, source_target_pairs={{0,12},{1,13},{2,14},{3,15},{4,0},{5,1},{6,2},{7,3},{8,4},{9,5},{1... | collective-permute-start | bytes 552968 | tf_op jit(solution)/shard_map/ppermute | solution.py:42
  55.2 4.0 %collective-permute-start.13 = (f32[360,128]{1,0:T(8,128)S(1)}, f32[360,128]{1,0:T(8,128)S(1)}, u32[]{:S(2)}, u32[]{:S(2)}) collective-permute-start(f32[360,128]{1,0:T(8,128)S(1)} %get-tuple-element.34), channel_id=1, source_target_pairs={{0,14},{1,15},{2,12},{3,13},{4,2},{5,3},{6,0},{7,1},{8,6},{9,7},{1... | collective-permute-start | bytes 552968 | tf_op jit(solution)/shard_map/ppermute | solution.py:42
  59.2 1.2 %shard_map.45 = (f32[32,11520]{1,0:T(8,128)}, f32[32,256]{1,0:T(8,128)S(1)}) custom-call(f32[360,128]{1,0:T(8,128)S(1)} %get-tuple-element.35.refs_0_, f32[360,128]{1,0:T(8,128)S(1)} %collective-permute-done.7.refs_1_, f32[360,128]{1,0:T(8,128)S(1)} %collective-permute-done.15.refs_2_, f32[360,128]{1,0:T(8,128)S(1)} %collective-permute-done.16.refs_3_, ...), custom_call_target="tpu_custom_call" | custom-call | bytes 3719168 | tf_op jit(solution)/shard_map/pallas_call | solution.py:244
  60.5 1.1 %collective-permute-done.10.m0.refs_0_ = f32[360,128]{1,0:T(8,128)S(1)} collective-permute-done((f32[360,128]{1,0:T(8,128)S(1)}, f32[360,128]{1,0:T(8,128)S(1)}, u32[]{:S(2)}, u32[]{:S(2)}) %collective-permute-start.10) | collective-permute-done | bytes 184352 | tf_op jit(solution)/shard_map/ppermute | solution.py:42
  61.5 2.8 %collective-permute-done.11.m1.refs_1_ = f32[360,128]{1,0:T(8,128)S(1)} collective-permute-done((f32[360,128]{1,0:T(8,128)S(1)}, f32[360,128]{1,0:T(8,128)S(1)}, u32[]{:S(2)}, u32[]{:S(2)}) %collective-permute-start.11) | collective-permute-done | bytes 184352 | tf_op jit(solution)/shard_map/ppermute | solution.py:42
  64.3 0.8 %shard_map.46.refs_6_ = f32[32,11520]{1,0:T(8,128)} custom-call(f32[360,128]{1,0:T(8,128)S(1)} %collective-permute-done.10.m0.refs_0_, f32[360,128]{1,0:T(8,128)S(1)} %collective-permute-done.11.m1.refs_1_, f32[32,11520]{1,0:T(8,128)S(1)} %copy-done, f32[32,11520]{1,0:T(8,128)} %get-tuple-element.40._), custom_call_target="tpu_custom_call", output_to_operand_aliasing={{}: (3, {})} | custom-call | bytes 1081344 | tf_op jit(solution)/shard_map/pallas_call | solution.py:230
  65.1 1.8 %collective-permute-done.13.refs_3_ = f32[360,128]{1,0:T(8,128)S(1)} collective-permute-done((f32[360,128]{1,0:T(8,128)S(1)}, f32[360,128]{1,0:T(8,128)S(1)}, u32[]{:S(2)}, u32[]{:S(2)}) %collective-permute-start.13) | collective-permute-done | bytes 184352 | tf_op jit(solution)/shard_map/ppermute | solution.py:42
  66.9 0.8 %shard_map.47 = f32[32,11520]{1,0:T(8,128)} custom-call(f32[360,128]{1,0:T(8,128)S(1)} %collective-permute-done.10.m0.refs_0_, f32[360,128]{1,0:T(8,128)S(1)} %collective-permute-done.11.m1.refs_1_, f32[360,128]{1,0:T(8,128)S(1)} %collective-permute-done.12.refs_2_, f32[360,128]{1,0:T(8,128)S(1)} %collective-permute-done.13.refs_3_, ...), custom_call_target="tpu_custom_call", output_to_operand_aliasing={{}: (6, {})} | custom-call | bytes 1081344 | tf_op jit(solution)/shard_map/pallas_call | solution.py:230
  (21 shorter events, 0.2 us)
Async XLA Ops:
  0.0 5.8 %collective-permute-start = (f32[2,512]{1,0:T(2,128)}, f32[2,512]{1,0:T(2,128)S(1)}, u32[]{:S(2)}, u32[]{:S(2)}) collective-permute-start(f32[2,512]{1,0:T(2,128)} %a.1), channel_id=1, source_target_pairs={{0,16},{1,17},{2,18},{3,19},{4,20},{5,21},{6,22},{7,23},{8,24},{9,... | collective-permute-start | bytes 12296 | tf_op jit(solution)/shard_map/ppermute | solution.py:50
  3.2 1.4 %copy-start.1 = (f32[32,11520]{1,0:T(8,128)S(1)}, f32[32,11520]{1,0:T(8,128)}, u32[]{:S(2)}) copy-start(f32[32,11520]{1,0:T(8,128)} %v.1) | copy-start | bytes 4423684
  5.8 5.4 %copy-start.2 = (f32[2,512]{1,0:T(2,128)S(1)}, f32[2,512]{1,0:T(2,128)}, u32[]{:S(2)}) copy-start(f32[2,512]{1,0:T(2,128)} %a.1) | copy-start | bytes 12292
  5.8 29.1 %all-to-all-start = ((f32[8,360,128]{2,1,0:T(8,128)}), f32[8,360,128]{2,1,0:T(8,128)S(1)}, u32[]{:S(2)}, u32[]{:S(2)}) async-start(f32[8,360,128]{2,1,0:T(8,128)} %shard_map.37), calls=%async_computation | async-start | bytes 2949120 | tf_op jit(solution)/shard_map/all_to_all | solution.py:38
  11.2 8.9 %collective-permute-start.1 = (f32[16,128]{1,0:T(8,128)S(1)}, f32[16,128]{1,0:T(8,128)S(1)}, u32[]{:S(2)}, u32[]{:S(2)}) collective-permute-start(f32[16,128]{1,0:T(8,128)S(1)} %shard_map.38.a), channel_id=1, source_target_pairs={{0,128},{1,129},{2,130},{3,131},{4,132},{5,133},{6,134},{7,135},{8... | collective-permute-start | bytes 24584 | tf_op jit(solution)/shard_map/ppermute | solution.py:50
  20.1 6.3 %collective-permute-start.2 = (f32[32,128]{1,0:T(8,128)S(1)}, f32[32,128]{1,0:T(8,128)S(1)}, u32[]{:S(2)}, u32[]{:S(2)}) collective-permute-start(f32[32,128]{1,0:T(8,128)S(1)} %shard_map.39.refs_0_), channel_id=1, source_target_pairs={{0,32},{1,33},{2,34},{3,35},{4,36},{5,37},{6,38},{7,39},{8,40},{9,... | collective-permute-start | bytes 49160 | tf_op jit(solution)/shard_map/ppermute | solution.py:50
  21.1 5.3 %collective-permute-start.3 = (f32[32,128]{1,0:T(8,128)S(1)}, f32[32,128]{1,0:T(8,128)S(1)}, u32[]{:S(2)}, u32[]{:S(2)}) collective-permute-start(f32[32,128]{1,0:T(8,128)S(1)} %shard_map.39.refs_0_), channel_id=1, source_target_pairs={{0,224},{1,225},{2,226},{3,227},{4,228},{5,229},{6,230},{7,231},{8... | collective-permute-start | bytes 49160 | tf_op jit(solution)/shard_map/ppermute | solution.py:50
  24.7 5.8 %collective-permute-start.4 = (f32[32,128]{1,0:T(8,128)S(1)}, f32[32,128]{1,0:T(8,128)S(1)}, u32[]{:S(2)}, u32[]{:S(2)}) collective-permute-start(f32[32,128]{1,0:T(8,128)S(1)} %shard_map.39.refs_0_), channel_id=1, source_target_pairs={{0,64},{1,193},{2,66},{3,195},{4,68},{5,197},{6,70},{7,199},{8,72}... | collective-permute-start | bytes 49160 | tf_op jit(solution)/shard_map/ppermute | solution.py:50
  30.6 4.4 %collective-permute-start.5 = (f32[128,128]{1,0:T(8,128)S(1)}, f32[128,128]{1,0:T(8,128)S(1)}, u32[]{:S(2)}, u32[]{:S(2)}) collective-permute-start(f32[128,128]{1,0:T(8,128)S(1)} %shard_map.40.a), channel_id=1, source_target_pairs={{0,2},{1,3},{2,0},{3,1},{4,6},{5,7},{6,4},{7,5},{8,10},{9,11},{10,... | collective-permute-start | bytes 196616 | tf_op jit(solution)/shard_map/ppermute | solution.py:42
  34.9 3.4 %collective-permute-start.6 = (f32[8,360,128]{2,1,0:T(8,128)S(1)}, f32[8,360,128]{2,1,0:T(8,128)S(1)}, u32[]{:S(2)}, u32[]{:S(2)}) collective-permute-start(f32[8,360,128]{2,1,0:T(8,128)S(1)} %all-to-all-done.mine), channel_id=1, source_target_pairs={{0,1},{1,0},{2,3},{3,2},{4,5},{5,4},{6,7},{7,6},{8,9},{9,8},{10,11... | collective-permute-start | bytes 4423688 | tf_op jit(solution)/shard_map/ppermute | solution.py:46
  35.0 8.5 %collective-permute-start.14 = (f32[256,128]{1,0:T(8,128)S(1)}, f32[256,128]{1,0:T(8,128)S(1)}, u32[]{:S(2)}, u32[]{:S(2)}) collective-permute-start(f32[256,128]{1,0:T(8,128)S(1)} %shard_map.41.amp), channel_id=1, source_target_pairs={{0,8},{1,9},{2,10},{3,11},{4,12},{5,13},{6,14},{7,15},{8,0},{9,1},... | collective-permute-start | bytes 393224 | tf_op jit(solution)/shard_map/ppermute | solution.py:42
  40.0 8.1 %collective-permute-start.7 = (f32[360,128]{1,0:T(8,128)S(1)}, f32[360,128]{1,0:T(8,128)S(1)}, u32[]{:S(2)}, u32[]{:S(2)}) collective-permute-start(f32[360,128]{1,0:T(8,128)S(1)} %get-tuple-element.28), channel_id=1, source_target_pairs={{0,2},{1,3},{2,0},{3,1},{4,6},{5,7},{6,4},{7,5},{8,10},{9,11},{10,... | collective-permute-start | bytes 552968 | tf_op jit(solution)/shard_map/ppermute | solution.py:42
  41.5 6.6 %collective-permute-start.8 = (f32[256,128]{1,0:T(8,128)S(1)}, f32[256,128]{1,0:T(8,128)S(1)}, u32[]{:S(2)}, u32[]{:S(2)}) collective-permute-start(f32[256,128]{1,0:T(8,128)S(1)} %shard_map.41.amp), channel_id=1, source_target_pairs={{0,4},{1,5},{2,6},{3,7},{4,8},{5,9},{6,10},{7,11},{8,12},{9,13},{1... | collective-permute-start | bytes 393224 | tf_op jit(solution)/shard_map/ppermute | solution.py:42
  42.9 5.1 %collective-permute-start.9 = (f32[256,128]{1,0:T(8,128)S(1)}, f32[256,128]{1,0:T(8,128)S(1)}, u32[]{:S(2)}, u32[]{:S(2)}) collective-permute-start(f32[256,128]{1,0:T(8,128)S(1)} %shard_map.41.amp), channel_id=1, source_target_pairs={{0,12},{1,13},{2,14},{3,15},{4,0},{5,1},{6,2},{7,3},{8,4},{9,5},{1... | collective-permute-start | bytes 393224 | tf_op jit(solution)/shard_map/ppermute | solution.py:42
  44.5 10.7 %collective-permute-start.15 = (f32[360,128]{1,0:T(8,128)S(1)}, f32[360,128]{1,0:T(8,128)S(1)}, u32[]{:S(2)}, u32[]{:S(2)}) collective-permute-start(f32[360,128]{1,0:T(8,128)S(1)} %get-tuple-element.37), channel_id=1, source_target_pairs={{0,8},{1,9},{2,10},{3,11},{4,12},{5,13},{6,14},{7,15},{8,0},{9,1},... | collective-permute-start | bytes 552968 | tf_op jit(solution)/shard_map/ppermute | solution.py:42
  46.6 12.7 %copy-start = (f32[32,11520]{1,0:T(8,128)S(1)}, f32[32,11520]{1,0:T(8,128)}, u32[]{:S(2)}) copy-start(f32[32,11520]{1,0:T(8,128)} %refs_4_.3) | copy-start | bytes 4423684
  46.6 12.7 %collective-permute-start.16 = (f32[360,128]{1,0:T(8,128)S(1)}, f32[360,128]{1,0:T(8,128)S(1)}, u32[]{:S(2)}, u32[]{:S(2)}) collective-permute-start(f32[360,128]{1,0:T(8,128)S(1)} %get-tuple-element.38), channel_id=1, source_target_pairs={{0,10},{1,11},{2,8},{3,9},{4,14},{5,15},{6,12},{7,13},{8,2},{9,3},... | collective-permute-start | bytes 552968 | tf_op jit(solution)/shard_map/ppermute | solution.py:42
  48.9 12.6 %collective-permute-start.10 = (f32[360,128]{1,0:T(8,128)S(1)}, f32[360,128]{1,0:T(8,128)S(1)}, u32[]{:S(2)}, u32[]{:S(2)}) collective-permute-start(f32[360,128]{1,0:T(8,128)S(1)} %get-tuple-element.31), channel_id=1, source_target_pairs={{0,4},{1,5},{2,6},{3,7},{4,8},{5,9},{6,10},{7,11},{8,12},{9,13},{1... | collective-permute-start | bytes 552968 | tf_op jit(solution)/shard_map/ppermute | solution.py:42
  50.6 13.7 %collective-permute-start.11 = (f32[360,128]{1,0:T(8,128)S(1)}, f32[360,128]{1,0:T(8,128)S(1)}, u32[]{:S(2)}, u32[]{:S(2)}) collective-permute-start(f32[360,128]{1,0:T(8,128)S(1)} %get-tuple-element.32), channel_id=1, source_target_pairs={{0,6},{1,7},{2,4},{3,5},{4,10},{5,11},{6,8},{7,9},{8,14},{9,15},{1... | collective-permute-start | bytes 552968 | tf_op jit(solution)/shard_map/ppermute | solution.py:42
  52.5 12.6 %collective-permute-start.12 = (f32[360,128]{1,0:T(8,128)S(1)}, f32[360,128]{1,0:T(8,128)S(1)}, u32[]{:S(2)}, u32[]{:S(2)}) collective-permute-start(f32[360,128]{1,0:T(8,128)S(1)} %get-tuple-element.33), channel_id=1, source_target_pairs={{0,12},{1,13},{2,14},{3,15},{4,0},{5,1},{6,2},{7,3},{8,4},{9,5},{1... | collective-permute-start | bytes 552968 | tf_op jit(solution)/shard_map/ppermute | solution.py:42
  55.2 11.7 %collective-permute-start.13 = (f32[360,128]{1,0:T(8,128)S(1)}, f32[360,128]{1,0:T(8,128)S(1)}, u32[]{:S(2)}, u32[]{:S(2)}) collective-permute-start(f32[360,128]{1,0:T(8,128)S(1)} %get-tuple-element.34), channel_id=1, source_target_pairs={{0,14},{1,15},{2,12},{3,13},{4,2},{5,3},{6,0},{7,1},{8,6},{9,7},{1... | collective-permute-start | bytes 552968 | tf_op jit(solution)/shard_map/ppermute | solution.py:42
